TPU v7x, 32 devices: a whole 2x2x4 slice. The times are simulated.
32 devices in a mesh: tile: 8 (over y, x, core), mp: 4 (over z).
Axes of the slice: x: 2, y: 2, z: 4, core: 2. Of those that a mesh axis runs over, the one named last changes fastest.
Arguments:
- tokens: bfloat16 [64, 256, 1024], P('tile', 'mp'), may hold values from -6 to 6
- ln_gain_one: float32 [1024], replicated, may hold values from 0.5 to 1.5
- ln_gain_two: float32 [1024], replicated, may hold values from 0.5 to 1.5
- qkv_weight: bfloat16 [3, 1024, 1024], P(None, None, 'mp'), may hold values from -2 to 2
- out_weight: bfloat16 [1024, 1024], P('mp'), may hold values from -0.1875 to 0.1875
- in_weight: bfloat16 [4096, 1024], P('mp'), may hold values from -0.1875 to 0.1875
- mlp_out_weight: bfloat16 [4096, 1024], P('mp'), may hold values from -0.09375 to 0.09375
- proj_weight: bfloat16 [1024, 256], replicated, may hold values from -0.1875 to 0.1875
- land_mask: int32 [64], P('tile'), may hold values 0 or 1
- placement: int32 [64], replicated, may hold values from 0 to 63, as said below
- guide: bfloat16 [256, 256, 256], P(('tile', 'mp')), may hold values from -6 to 6
- conv_weights: bfloat16 [3, 3, 3, 256, 256], replicated, may hold values from -0.125 to 0.125
- conv_bias: float32 [3, 256], replicated, may hold values from -3 to 3
Outputs:
- dense_map: bfloat16 [256, 256, 256], P(('tile', 'mp'))
Inputs may be any that keep to these rules, and one draw needn't show every extreme that they name: placement is a permutation of the scene positions; the tiles of one group land in different slabs (entry // 8), so each slab receives at most one tile of each group.
All inputs are finite; a program needn't handle non-finite values. No bound on the sum of `land_mask` on one device may be relied on, other than what follows from the above.
Results may differ from a plain program's by a relative error of at most 0.018.
The roundings to bfloat16 on the way count: a program that leaves them out, or rounds other values in their place, can miss the bound.
Values may be sent and summed in bfloat16 or wider, within the bound.
A program may use at most 128 MiB of HBM per device.

v0:
```python
import functools

import jax
import jax.numpy as jnp
from jax import lax
from jax.experimental import pallas as pl
from jax.experimental.pallas import tpu as pltpu
from jax.sharding import PartitionSpec as P

HEAD = 64
SIDE = 16
UP = 2
PATCHES = 256
HALO = 3
PLANE = 8
KINDS = 10


def layer_norm(values, gain):
    widened = values.astype(jnp.float32)
    centre = jnp.mean(widened, axis=-1, keepdims=True)
    spread = jnp.mean((widened - centre) ** 2, axis=-1, keepdims=True)
    return ((widened - centre) * lax.rsqrt(spread + 1e-06) * gain).astype(jnp.bfloat16)


def flip(index, bit):
    return index + bit - 2 * bit * (index // bit % 2)


def gather_kernel(
    count,
    tiles_each,
    tokens_ref,
    qkv_ref,
    out_ref,
    in_ref,
    mlp_ref,
    seq_ref,
    qkv_all,
    out_all,
    in_all,
    mlp_all,
    token_send,
    token_recv,
    own_sem,
    chain_send,
    send_sem,
    recv_sem,
):
    me_t = lax.axis_index("tile")
    me_z = lax.axis_index("mp")
    seg = tokens_ref.shape[1]
    shards = (qkv_ref, out_ref, in_ref, mlp_ref)
    gathered = (qkv_all, out_all, in_all, mlp_all)

    barrier = pltpu.get_barrier_semaphore()
    for bit in (1, 2, 4):
        pl.semaphore_signal(
            barrier, inc=1, device_id={"tile": flip(me_t, bit), "mp": me_z},
            device_id_type=pl.DeviceIdType.MESH,
        )
    for step in range(1, count):
        pl.semaphore_signal(
            barrier, inc=1, device_id={"tile": me_t, "mp": lax.rem(me_z + step, count)},
            device_id_type=pl.DeviceIdType.MESH,
        )
    pl.semaphore_wait(barrier, 3 + count - 1)

    def piece(which, origin, owner, part=None):
        rows = gathered[which].shape[1] // PLANE
        cols = gathered[which].shape[2]
        begin = pl.multiple_of(owner % PLANE * rows, rows)
        if part is None:
            return (origin, pl.ds(begin, rows))
        if rows % 32 == 0:
            half = rows // 2
            return (origin, pl.ds(pl.multiple_of(begin + part * half, half), half))
        half = cols // 2
        return (origin, pl.ds(begin, rows), pl.ds(part * half, half))

    def remote(src, dst, send, recv, tile, mp):
        return pltpu.make_async_remote_copy(
            src_ref=src, dst_ref=dst, send_sem=send, recv_sem=recv,
            device_id={"tile": tile, "mp": mp}, device_id_type=pl.DeviceIdType.MESH,
        )

    token_copies = []
    for step in range(1, count):
        target = lax.rem(me_z + step, count)
        copy = remote(
            tokens_ref.at[pl.ds(target * tiles_each, tiles_each)],
            seq_ref.at[:, pl.ds(pl.multiple_of(me_z * seg, seg), seg)],
            token_send.at[step], token_recv.at[step], me_t, target,
        )
        copy.start()
        token_copies.append(copy)
    own_tokens = pltpu.make_async_copy(
        tokens_ref.at[pl.ds(me_z * tiles_each, tiles_each)],
        seq_ref.at[:, pl.ds(pl.multiple_of(me_z * seg, seg), seg)],
        token_send.at[0],
    )
    own_tokens.start()

    def chain(which, origin, src, up):
        slot = 1 if up else 0
        target = me_z + 1 if up else me_z - 1
        ref = src
        return remote(
            ref, gathered[which].at[piece(which, origin, me_t)],
            chain_send.at[which, origin, slot], recv_sem.at[which, origin, 0], me_t, target,
        )

    def own_piece(which):
        rows = shards[which].shape[0] // PLANE
        return shards[which].at[pl.ds(pl.multiple_of(me_t % PLANE * rows, rows), rows)]

    def first_sends(which, wait):
        for up in (True, False):
            @pl.when(me_z + 1 < count if up else me_z > 0)
            def _():
                copy = chain(which, me_z, own_piece(which), up)
                if wait:
                    copy.wait_send()
                else:
                    copy.start()

    def source(index):
        below, above = me_z, count - 1 - me_z
        least = jnp.minimum(below, above)
        paired = index < 2 * least
        down_side = jnp.where(paired, index % 2 == 0, below > above)
        far = jnp.where(paired, index // 2 + 1, index - least + 1)
        return jnp.where(down_side, me_z - far, me_z + far), down_side

    def ring(which, origin, owner, kind, part, bit):
        where = piece(which, origin, owner, part)
        ref = gathered[which].at[where]
        return remote(
            ref, ref, send_sem.at[which, origin, kind], recv_sem.at[which, origin, kind],
            flip(me_t, bit), me_z,
        )

    def routes(device):
        first_bit = 2 + 2 * (device % 2)
        second_bit = 4 - 2 * (device % 2)
        first_of, second_of = flip(device, first_bit), flip(device, second_bit)
        both = flip(flip(device, 2), 4)
        return {
            1: (device, None, first_bit),
            2: (device, None, second_bit),
            3: (first_of, 0, second_bit),
            4: (second_of, 1, first_bit),
            5: (device, None, 1),
            6: (first_of, None, 1),
            7: (second_of, None, 1),
            8: (both, 0, 1),
            9: (both, 1, 1),
        }

    outward = routes(me_t)
    inward = routes(flip(me_t, 1))

    def go(which, origin, kind):
        owner, part, bit = outward[kind]
        ring(which, origin, owner, kind, part, bit).start()

    def arrived(which, origin, kind):
        owner, part, bit = (outward if kind < 5 else inward)[kind]
        if kind < 5:
            owner = flip(owner, bit)
        ring(which, origin, owner, kind, part, bit).wait_recv()

    def stage_a(which, index):
        origin, down_side = source(index)
        chain(which, origin, gathered[which].at[piece(which, origin, me_t)], True).wait_recv()
        for up in (True, False):
            @pl.when((down_side & (me_z + 1 < count)) if up else
                     (jnp.logical_not(down_side) & (me_z > 0)))
            def _():
                chain(which, origin, gathered[which].at[piece(which, origin, me_t)], up).start()
        go(which, origin, 1)
        go(which, origin, 2)
        go(which, origin, 5)

    def stage_b(which, index):
        origin, _ = source(index)
        arrived(which, origin, 1)
        go(which, origin, 3)
        go(which, origin, 6)
        arrived(which, origin, 2)
        go(which, origin, 4)
        go(which, origin, 7)

    def stage_c(which, index):
        origin, _ = source(index)
        arrived(which, origin, 3)
        go(which, origin, 8)
        arrived(which, origin, 4)
        go(which, origin, 9)

    def stage_d(which, index):
        origin, _ = source(index)
        for kind in (5, 6, 7, 8, 9):
            arrived(which, origin, kind)

    own_copies = [
        pltpu.make_async_copy(shards[which], gathered[which].at[me_z], own_sem.at[which])
        for which in range(4)
    ]
    first_sends(0, False)
    for copy in own_copies:
        copy.start()
    first_sends(1, False)

    units = [(which, index) for which in range(4) for index in range(count - 1)]
    stages = (stage_a, stage_b, stage_c)
    for tick in range(len(units) + 2):
        for late, stage in enumerate(stages):
            at = tick - late
            if 0 <= at < len(units):
                stage(*units[at])
                if late == 0 and units[at][1] == 0 and units[at][0] + 2 < 4:
                    first_sends(units[at][0] + 2, False)

    for which, index in units:
        stage_d(which, index)
    own_tokens.wait()
    for copy in token_copies:
        copy.wait()
    for copy in own_copies:
        copy.wait()
    for which in range(4):
        first_sends(which, True)
        for index in range(count - 1):
            origin, down_side = source(index)
            for up in (True, False):
                @pl.when((down_side & (me_z + 1 < count)) if up else
                         (jnp.logical_not(down_side) & (me_z > 0)))
                def _():
                    chain(
                        which, origin, gathered[which].at[piece(which, origin, me_t)], up
                    ).wait_send()
            for kind in range(1, KINDS):
                owner, part, bit = outward[kind]
                ring(which, origin, owner, kind, part, bit).wait_send()


def gather_all(tokens, qkv, out, into, mlp):
    count = lax.axis_size("mp")
    tiles_each = tokens.shape[0] // count
    any_space = pl.BlockSpec(memory_space=pl.ANY)
    return pl.pallas_call(
        functools.partial(gather_kernel, count, tiles_each),
        out_shape=(
            jax.ShapeDtypeStruct((tiles_each, PATCHES, tokens.shape[2]), jnp.bfloat16),
        ) + tuple(
            jax.ShapeDtypeStruct((count,) + part.shape, jnp.bfloat16)
            for part in (qkv, out, into, mlp)
        ),
        in_specs=[any_space] * 5,
        out_specs=(any_space,) * 5,
        scratch_shapes=[
            pltpu.SemaphoreType.DMA((count,)),
            pltpu.SemaphoreType.DMA((count,)),
            pltpu.SemaphoreType.DMA((4,)),
            pltpu.SemaphoreType.DMA((4, count, 2)),
            pltpu.SemaphoreType.DMA((4, count, KINDS)),
            pltpu.SemaphoreType.DMA((4, count, KINDS)),
        ],
        compiler_params=pltpu.CompilerParams(collective_id=0, has_side_effects=True),
        name="gather_weights",
    )(tokens, qkv, out, into, mlp)


def neighbours(block, width, dim=0):
    axes = ("tile", "mp")
    count = lax.axis_size(axes)
    forward = [(i, i + 1) for i in range(count - 1)]
    backward = [(target, source) for source, target in forward]
    low = lax.ppermute(lax.slice_in_dim(block, block.shape[dim] - width, None, axis=dim), axes, forward)
    high = lax.ppermute(lax.slice_in_dim(block, 0, width, axis=dim), axes, backward)
    return low, high


def scene_kernel(
    row_count,
    scene_rows,
    low_ref,
    mid_ref,
    high_ref,
    guide_low,
    guide_mid,
    guide_high,
    weights_ref,
    bias_ref,
    result_ref,
    guided_buf,
    first_buf,
    second_buf,
):
    here = lax.axis_index(("tile", "mp"))
    width_px, channels = guide_mid.shape[1:]
    cols = width_px // UP
    column = lax.broadcasted_iota(jnp.int32, (width_px, channels), 0)
    spread = (
        lax.broadcasted_iota(jnp.int32, (width_px, cols), 0) // UP
        == lax.broadcasted_iota(jnp.int32, (width_px, cols), 1)
    ).astype(jnp.bfloat16)

    def put(buffer, row, values):
        before = jnp.where(column == 0, 0.0, pltpu.roll(values, 1, 0))
        after = jnp.where(column == width_px - 1, 0.0, pltpu.roll(values, width_px - 1, 0))
        buffer[row, :, pl.ds(0, channels)] = before.astype(jnp.bfloat16)
        buffer[row, :, pl.ds(channels, channels)] = values.astype(jnp.bfloat16)
        buffer[row, :, pl.ds(2 * channels, channels)] = after.astype(jnp.bfloat16)

    def token_row(row):
        inner = mid_ref.shape[1] // SIDE
        if row < UP:
            ref, at = low_ref, row
        elif row < UP + inner:
            ref, at = mid_ref, row - UP
        else:
            ref, at = high_ref, row - UP - inner
        line = ref[:, pl.ds(at * SIDE, SIDE), :].reshape(cols, channels)
        return jnp.dot(spread, line, preferred_element_type=jnp.float32)

    def guide_row(row):
        if row < HALO:
            return guide_low[row]
        if row < HALO + row_count:
            return guide_mid[row - HALO]
        return guide_high[row - HALO - row_count]

    for row in range(row_count + 2 * HALO):
        put(guided_buf, row, token_row((row + 1) // UP) + guide_row(row).astype(jnp.float32))

    def conv(buffer, layer, row):
        total = jnp.zeros((2 * width_px, channels), jnp.float32) + bias_ref[pl.ds(layer, 1), :]
        for shift in range(3):
            window = buffer[pl.ds(row + shift, 2)].reshape(2 * width_px, 3 * channels)
            total += jnp.dot(window, weights_ref[layer, shift], preferred_element_type=jnp.float32)
        return total

    for layer, source, target in ((0, guided_buf, first_buf), (1, first_buf, second_buf)):
        reach = HALO - 1 - layer

        @pl.loop(0, row_count // 2 + reach)
        def _(pair):
            values = jax.nn.gelu(conv(source, layer, 2 * pair))
            for part in range(2):
                at = here * row_count - reach + 2 * pair + part
                keep = (at >= 0) & (at < scene_rows)
                line = values[part * width_px : (part + 1) * width_px]
                put(target, 2 * pair + part, jnp.where(keep, line, 0.0))

    @pl.loop(0, row_count // 2)
    def _(pair):
        values = conv(second_buf, 2, 2 * pair).reshape(2, width_px, channels)
        base = guided_buf[pl.ds(2 * pair + HALO, 2), :, pl.ds(channels, channels)]
        result_ref[pl.ds(2 * pair, 2)] = (base.astype(jnp.float32) + values).astype(jnp.bfloat16)


def scene(slab, guide, guide_low, guide_high, conv_weights, conv_bias):
    rows, width_px, channels = guide.shape
    ring = lax.axis_size(("tile", "mp"))
    low, high = neighbours(slab, UP * SIDE, 1)
    weights = conv_weights.reshape(3, 3, 3 * channels, channels)
    return pl.pallas_call(
        functools.partial(scene_kernel, rows, rows * ring),
        out_shape=jax.ShapeDtypeStruct(guide.shape, jnp.bfloat16),
        in_specs=[pl.BlockSpec(memory_space=pltpu.VMEM)] * 8,
        out_specs=pl.BlockSpec(memory_space=pltpu.VMEM),
        scratch_shapes=[
            pltpu.VMEM((rows + 2 * reach, width_px, 3 * channels), jnp.bfloat16)
            for reach in (3, 2, 1)
        ],
        compiler_params=pltpu.CompilerParams(vmem_limit_bytes=50 << 20),
        name="scene_convolutions",
    )(low, slab, high, guide_low, guide, guide_high, weights, conv_bias)


def per_device(
    tokens,
    ln_gain_one,
    ln_gain_two,
    qkv_weight,
    out_weight,
    in_weight,
    mlp_out_weight,
    proj_weight,
    land_mask,
    placement,
    guide,
    conv_weights,
    conv_bias,
):
    tiles_here, seg_rows, width = tokens.shape
    groups = lax.axis_size("tile")
    parts = lax.axis_size("mp")
    tiles_each = tiles_here // parts
    guide_low, guide_high = neighbours(guide, HALO)

    heads_local = qkv_weight.shape[2] // HEAD
    seq, qkv_all, out_all, in_all, mlp_all = gather_all(
        tokens, qkv_weight.reshape(-1, qkv_weight.shape[2]), out_weight, in_weight, mlp_out_weight
    )
    qkv_all = qkv_all.reshape(parts, 3, width, heads_local * HEAD)
    out_all = out_all.reshape(-1, width)
    in_all = in_all.reshape(-1, width)
    mlp_all = mlp_all.reshape(-1, width)

    normed = layer_norm(seq, ln_gain_one)
    projected = jnp.einsum(
        "tpd,zkde->kztpe", normed, qkv_all, preferred_element_type=jnp.float32
    ).astype(jnp.bfloat16)
    shaped = projected.reshape(3, parts, tiles_each, PATCHES, heads_local, HEAD)
    scores = jnp.einsum(
        "ztphe,ztqhe->zthpq", shaped[0], shaped[1], preferred_element_type=jnp.float32
    ) * HEAD ** (-0.5)
    soft_weights = jax.nn.softmax(scores, axis=-1).astype(jnp.bfloat16)
    context = jnp.einsum(
        "zthpq,ztqhe->tpzhe", soft_weights, shaped[2], preferred_element_type=jnp.float32
    )
    context = context.astype(jnp.bfloat16).reshape(tiles_each, PATCHES, width)
    attention = jnp.einsum("tpe,ed->tpd", context, out_all, preferred_element_type=jnp.float32)
    middle = (seq.astype(jnp.float32) + attention).astype(jnp.bfloat16)
    normed_mid = layer_norm(middle, ln_gain_two)
    hidden = jnp.einsum("tpd,fd->tpf", normed_mid, in_all, preferred_element_type=jnp.float32)
    hidden = jax.nn.gelu(hidden).astype(jnp.bfloat16)
    mlp_part = jnp.einsum("tpf,fd->tpd", hidden, mlp_all, preferred_element_type=jnp.float32)
    features = (middle.astype(jnp.float32) + mlp_part).astype(jnp.bfloat16)
    mask_here = lax.dynamic_slice_in_dim(
        land_mask, lax.axis_index("mp") * tiles_each, tiles_each, 0
    ).astype(jnp.bfloat16)
    embed = jnp.einsum("tpd,dc->tpc", features, proj_weight, preferred_element_type=jnp.float32)
    embed = embed.astype(jnp.bfloat16) * mask_here[:, None, None]
    channels = embed.shape[-1]

    split = embed.reshape(tiles_each, parts, seg_rows, channels).transpose(1, 0, 2, 3)
    split = lax.all_to_all(split, "mp", split_axis=0, concat_axis=0, tiled=True)
    split = split.reshape(tiles_here, seg_rows, channels)

    group_here = lax.axis_index("tile")
    slab_all = placement // tiles_here
    column_all = placement % tiles_here
    group_all = jnp.arange(placement.shape[0], dtype=jnp.int32) // tiles_here
    slab_local = lax.dynamic_slice_in_dim(slab_all, group_here * tiles_here, tiles_here, 0)
    selector = (slab_local[None, :] == jnp.arange(groups, dtype=jnp.int32)[:, None]).astype(
        jnp.bfloat16
    )
    in_slab = slab_all == group_here
    column_hot = (
        column_all[:, None] == jnp.arange(tiles_here, dtype=jnp.int32)[None, :]
    ) & in_slab[:, None]
    group_hot = group_all[:, None] == jnp.arange(groups, dtype=jnp.int32)[None, :]
    arrange = jnp.einsum(
        "tk,tg->kg", column_hot.astype(jnp.float32), group_hot.astype(jnp.float32)
    ).astype(jnp.bfloat16)
    outgoing = jnp.einsum(
        "sj,jpd->spd", selector, split, preferred_element_type=jnp.float32
    ).astype(jnp.bfloat16)
    incoming = lax.all_to_all(outgoing, "tile", split_axis=0, concat_axis=0, tiled=True)
    slab_embed = jnp.einsum(
        "kg,gpd->kpd", arrange, incoming, preferred_element_type=jnp.float32
    ).astype(jnp.bfloat16)
    return scene(slab_embed, guide, guide_low, guide_high, conv_weights, conv_bias)


def solution(mesh):
    in_specs = (
        P("tile", "mp", None),
        P(),
        P(),
        P(None, None, "mp"),
        P("mp", None),
        P("mp", None),
        P("mp", None),
        P(),
        P("tile"),
        P(),
        P(("tile", "mp"), None, None),
        P(),
        P(),
    )
    out_specs = P(("tile", "mp"), None, None)
    return jax.shard_map(
        per_device, mesh=mesh, in_specs=in_specs, out_specs=out_specs, check_vma=False
    )
```

profile of v0, /device:TPU:0, one launch (start us, length us, event | category | flops | bytes accessed | tf_op | source)
XLA Modules:
  0.0 314.3 jit_solution(12556751687877379287)
XLA Ops:
  0.0 0.0 copy-start
  0.0 0.0 copy-start.6
  0.0 208.1 %gather_weights.1 = (bf16[2,256,1024]{2,1,0:T(8,128)(2,1)}, bf16[4,3072,256]{2,1,0:T(8,128)(2,1)}, bf16[4,256,1024]{2,1,0:T(8,128)(2,1)}, bf16[4,1024,1024]{2,1,0:T(8,128)(2,1)}, bf16[4,1024,1024]{2,1,0:T(8,128)(2,1)}) custom-call(bf16[8,64,1024]{2,1,0:T(8,128)(2,1)} %tokens_ref.1, bf16[3072,256]{1,0:T(8,128)(2,1)} %bitcast.55, bf16[256,1024]{1,0:T(8,128)(2,1)} %out_ref.1, ...), custom_call_target="tpu_custom_call" | custom-call | tf_op jit(solution)/shard_map/gather_weights/pallas_call | solution.py:252
  208.2 1.4 convert_reduce_fusion.1
  209.6 1.6 fusion.22
  211.3 0.0 copy-done.6
  211.3 6.7 %convert_bitcast_fusion = bf16[3,4,2,256,256]{3,4,2,0,1:T(8,128)(2,1)S(1)} fusion(bf16[4,3,1024,256,1]{3,2,4,1,0:T(8,128)(2,1)} %bitcast.63, bf16[2,256,1024]{2,1,0:T(8,128)(2,1)} %get-tuple-element.10, f32[1024]{0:T(1024)S(1)} %copy-done.6, f32[2,256]{1,0:T(2,128)S(1)} %add_rsqrt_fusion.1, f32[2,256]{1,0:T(2,128)S(1)} %broadcast_multiply_fusion.1), kind=kOutput, calls=%fused_computation.20 | convolution fusion | flops 3225419776 | bytes 10493952 | tf_op jit(solution)/shard_map/tpd,zkde->kztpe/dot_general | solution.py:414
  218.0 1.2 fusion.69
  219.2 7.4 %fusion.72 = (f32[4,2,4,256]{3,2,1,0:T(4,128)S(1)}, f32[4,2,4,256,256]{3,4,2,1,0:T(8,128)}) fusion(bf16[4,2,256,4,64]{2,4,3,1,0:T(8,128)(2,1)} %bitcast.59, bf16[4,2,256,4,64]{2,4,3,1,0:T(8,128)(2,1)S(1)} %bitcast.58), kind=kOutput, calls=%fused_computation.89 | convolution fusion | flops 274727168 | bytes 10518528 | tf_op jit(solution)/shard_map/sub | solution.py:421
  226.6 0.0 copy-start.5
  226.6 4.4 %fusion.27 = bf16[2,4,4,64,256]{4,3,2,1,0:T(8,128)(2,1)S(1)} fusion(bf16[4,2,256,4,64]{2,4,3,1,0:T(8,128)(2,1)S(1)} %bitcast.57, f32[4,2,4,256,256]{3,4,2,1,0:T(8,128)} %get-tuple-element.25, f32[4,2,4,256]{3,2,1,0:T(4,128)S(1)} %get-tuple-element.24), kind=kOutput, calls=%fused_computation.36 | convolution fusion | flops 273154048 | bytes 10518528 | tf_op jit(solution)/shard_map/zthpq,ztqhe->tpzhe/dot_general | solution.py:422
  231.0 0.0 copy-done.3
  231.0 0.0 copy-done.5
  231.0 0.0 copy-start.8
  231.0 0.0 copy-start.7
  231.0 1.4 convert_reduce_fusion
  232.4 0.4 fusion.19
  232.8 0.0 copy-done.8
  232.8 0.1 dynamic-slice_convert_fusion
  232.9 0.0 copy-done.7
  232.9 0.0 copy-start.4
  232.9 15.3 %fusion.26 = bf16[2,256,1024]{2,1,0:T(8,128)(2,1)S(1)} fusion(bf16[2,256,1024]{2,1,0:T(8,128)(2,1)S(1)} %get-tuple-element.27, bf16[4096,1024,1]{1,0,2:T(8,128)(2,1)} %bitcast.62, bf16[4096,1024,1]{1,0,2:T(8,128)(2,1)} %bitcast.61, f32[1024]{0:T(1024)S(1)} %copy-done.7, f32[2,256]{1,0:T(2,128)S(1)} %add_rsqrt_fusion, f32[2,256]{1,0:T(2,128)S(1)} %broadcast_multiply_fusion), kind=kOutput, calls=%fused_computation.35 | convolution fusion | flops 8613003264 | bytes 18882560 | tf_op jit(solution)/shard_map/tpf,fd->tpd/dot_general | solution.py:431
  248.2 0.0 copy-done
  248.2 0.0 copy-start.1
  248.2 0.0 copy-start.2
  248.2 0.4 fusion.30
  248.7 0.7 copy.54
  249.4 3.4 %all-to-all-start = ((bf16[4,2,64,256]{3,2,1,0:T(8,128)(2,1)}), bf16[4,2,64,256]{3,2,1,0:T(8,128)(2,1)S(1)}, u32[]{:S(2)}, u32[]{:S(2)}) async-start(bf16[4,2,64,256]{3,2,1,0:T(8,128)(2,1)} %bitcast.53), calls=%async_computation | async-start | bytes 524288 | tf_op jit(solution)/shard_map/all_to_all | solution.py:441
  252.8 0.0 copy-done.4
  252.8 0.1 dynamic_slice.6
  252.9 8.8 %all-to-all-done = bf16[4,2,64,256]{3,2,1,0:T(8,128)(2,1)S(1)} async-done(((bf16[4,2,64,256]{3,2,1,0:T(8,128)(2,1)}), bf16[4,2,64,256]{3,2,1,0:T(8,128)(2,1)S(1)}, u32[]{:S(2)}, u32[]{:S(2)}) %all-to-all-start) | async-done | bytes 262176 | tf_op jit(solution)/shard_map/all_to_all | solution.py:441
  261.7 0.2 convolution_convert_fusion
  261.9 0.8 copy.31
  262.7 3.7 %all-to-all-start.1 = ((bf16[8,64,256]{2,1,0:T(8,128)(2,1)}), bf16[8,64,256]{2,1,0:T(8,128)(2,1)S(1)}, u32[]{:S(2)}, u32[]{:S(2)}) async-start(bf16[8,64,256]{2,1,0:T(8,128)(2,1)} %copy.31), calls=%async_computation.1 | async-start | bytes 524288 | tf_op jit(solution)/shard_map/all_to_all | solution.py:463
  266.4 0.0 copy-done.1
  266.4 0.8 fusion.70
  267.2 2.1 collective-permute-start.2
  269.3 1.3 collective-permute-start.3
  270.6 2.7 all-to-all-done.1
  273.3 0.5 fusion.48
  273.9 2.1 collective-permute-start
  276.0 1.3 collective-permute-start.1
  277.3 1.8 collective-permute-done.2.guide_low
  279.1 13.1 %collective-permute-done.3.guide_high = bf16[3,256,256]{2,1,0:T(8,128)(2,1)S(1)} collective-permute-done((bf16[3,256,256]{2,1,0:T(8,128)(2,1)S(1)}, bf16[3,256,256]{2,1,0:T(8,128)(2,1)S(1)}, u32[]{:S(2)}, u32[]{:S(2)}) %collective-permute-start.3) | collective-permute-done | bytes 393248 | tf_op jit(solution)/shard_map/ppermute | solution.py:281
  292.2 0.0 collective-permute-done.low_ref
  292.2 4.4 %collective-permute-done.1.high_ref = bf16[8,32,256]{2,1,0:T(8,128)(2,1)S(1)} collective-permute-done((bf16[8,32,256]{2,1,0:T(8,128)(2,1)S(1)}, bf16[8,32,256]{2,1,0:T(8,128)(2,1)S(1)}, u32[]{:S(2)}, u32[]{:S(2)}) %collective-permute-start.1) | collective-permute-done | bytes 131104 | tf_op jit(solution)/shard_map/ppermute | solution.py:281
  296.6 0.0 copy-done.2
  296.6 17.8 %scene_convolutions.1 = bf16[8,256,256]{2,1,0:T(8,128)(2,1)} custom-call(bf16[8,32,256]{2,1,0:T(8,128)(2,1)S(1)} %collective-permute-done.low_ref, bf16[8,64,256]{2,1,0:T(8,128)(2,1)S(1)} %copy.53.mid_ref, bf16[8,32,256]{2,1,0:T(8,128)(2,1)S(1)} %collective-permute-done.1.high_ref, bf16[3,256,256]{2,1,0:T(8,128)(2,1)S(1)} %collective-permute-done.2.guide_low, ...), custom_call_target="tpu_custom_call" | custom-call | tf_op jit(solution)/shard_map/scene_convolutions/pallas_call | solution.py:369
  (9 shorter events, 0.1 us)
Async XLA Ops:
  0.0 248.2 %copy-start = (bf16[1024,256]{1,0:T(8,128)(2,1)S(1)}, bf16[1024,256]{1,0:T(8,128)(2,1)}, u32[]{:S(2)}) copy-start(bf16[1024,256]{1,0:T(8,128)(2,1)} %param.20) | copy-start | bytes 1572868
  0.0 211.3 %copy-start.6 = (f32[1024]{0:T(1024)S(1)}, f32[1024]{0:T(1024)}, u32[]{:S(2)}) copy-start(f32[1024]{0:T(1024)} %param.14) | copy-start | bytes 12292
  226.6 4.4 %copy-start.3 = (bf16[2,256,1024]{2,1,0:T(8,128)(2,1)S(1)}, bf16[2,256,1024]{2,1,0:T(8,128)(2,1)}, u32[]{:S(2)}) copy-start(bf16[2,256,1024]{2,1,0:T(8,128)(2,1)} %get-tuple-element.10) | copy-start | bytes 3145732
  226.6 4.4 %copy-start.5 = (bf16[4,256,1024]{2,1,0:T(8,128)(2,1)S(1)}, bf16[4,256,1024]{2,1,0:T(8,128)(2,1)}, u32[]{:S(2)}) copy-start(bf16[4,256,1024]{2,1,0:T(8,128)(2,1)} %get-tuple-element.12) | copy-start | bytes 6291460
  231.0 1.8 copy-start.8
  231.0 1.9 copy-start.7
  232.9 19.9 %copy-start.4 = (s32[64]{0:T(128)S(1)}, s32[64]{0:T(128)}, u32[]{:S(2)}) copy-start(s32[64]{0:T(128)} %param.22) | copy-start | bytes 772
  248.2 18.2 %copy-start.1 = (bf16[8,256,256]{2,1,0:T(8,128)(2,1)S(1)}, bf16[8,256,256]{2,1,0:T(8,128)(2,1)}, u32[]{:S(2)}) copy-start(bf16[8,256,256]{2,1,0:T(8,128)(2,1)} %guide_mid.1) | copy-start | bytes 3145732
  248.2 48.4 %copy-start.2 = (f32[3,256]{1,0:T(4,128)S(1)}, f32[3,256]{1,0:T(4,128)}, u32[]{:S(2)}) copy-start(f32[3,256]{1,0:T(4,128)} %bias_ref.1) | copy-start | bytes 9220
  249.4 12.3 %all-to-all-start = ((bf16[4,2,64,256]{3,2,1,0:T(8,128)(2,1)}), bf16[4,2,64,256]{3,2,1,0:T(8,128)(2,1)S(1)}, u32[]{:S(2)}, u32[]{:S(2)}) async-start(bf16[4,2,64,256]{3,2,1,0:T(8,128)(2,1)} %bitcast.53), calls=%async_computation | async-start | bytes 524288 | tf_op jit(solution)/shard_map/all_to_all | solution.py:441
  262.7 10.7 %all-to-all-start.1 = ((bf16[8,64,256]{2,1,0:T(8,128)(2,1)}), bf16[8,64,256]{2,1,0:T(8,128)(2,1)S(1)}, u32[]{:S(2)}, u32[]{:S(2)}) async-start(bf16[8,64,256]{2,1,0:T(8,128)(2,1)} %copy.31), calls=%async_computation.1 | async-start | bytes 524288 | tf_op jit(solution)/shard_map/all_to_all | solution.py:463
  267.2 11.9 %collective-permute-start.2 = (bf16[3,256,256]{2,1,0:T(8,128)(2,1)}, bf16[3,256,256]{2,1,0:T(8,128)(2,1)S(1)}, u32[]{:S(2)}, u32[]{:S(2)}) collective-permute-start(bf16[3,256,256]{2,1,0:T(8,128)(2,1)} %get-tuple-element.21), channel_id=1, source_target_pairs={{0,1},{1,2},{2,3},{3,4},{4,5},{5,6},{6,7},{7,8},{8,9},{9,10},{10,1... | collective-permute-start | bytes 1179656 | tf_op jit(solution)/shard_map/ppermute | solution.py:280
  269.3 22.9 %collective-permute-start.3 = (bf16[3,256,256]{2,1,0:T(8,128)(2,1)S(1)}, bf16[3,256,256]{2,1,0:T(8,128)(2,1)S(1)}, u32[]{:S(2)}, u32[]{:S(2)}) collective-permute-start(bf16[3,256,256]{2,1,0:T(8,128)(2,1)S(1)} %get-tuple-element.20), channel_id=1, source_target_pairs={{1,0},{2,1},{3,2},{4,3},{5,4},{6,5},{7,6},{8,7},{9,8},{10,9},{11,1... | collective-permute-start | bytes 1179656 | tf_op jit(solution)/shard_map/ppermute | solution.py:281
  273.9 18.3 %collective-permute-start = (bf16[8,32,256]{2,1,0:T(8,128)(2,1)S(1)}, bf16[8,32,256]{2,1,0:T(8,128)(2,1)S(1)}, u32[]{:S(2)}, u32[]{:S(2)}) collective-permute-start(bf16[8,32,256]{2,1,0:T(8,128)(2,1)S(1)} %get-tuple-element.23), channel_id=1, source_target_pairs={{0,1},{1,2},{2,3},{3,4},{4,5},{5,6},{6,7},{7,8},{8,9},{9,10},{10,1... | collective-permute-start | bytes 393224 | tf_op jit(solution)/shard_map/ppermute | solution.py:280
  276.0 20.6 %collective-permute-start.1 = (bf16[8,32,256]{2,1,0:T(8,128)(2,1)S(1)}, bf16[8,32,256]{2,1,0:T(8,128)(2,1)S(1)}, u32[]{:S(2)}, u32[]{:S(2)}) collective-permute-start(bf16[8,32,256]{2,1,0:T(8,128)(2,1)S(1)} %get-tuple-element.22), channel_id=1, source_target_pairs={{1,0},{2,1},{3,2},{4,3},{5,4},{6,5},{7,6},{8,7},{9,8},{10,9},{11,1... | collective-permute-start | bytes 393224 | tf_op jit(solution)/shard_map/ppermute | solution.py:281
where the time goes:
time: 315 us; the launch traced here: 314 us
  Pallas kernels  226 us (72%)
  matrix products  36.2 us (11%)
  waiting for transfers between devices  30.8 us (10%)
  starting transfers between devices  13.9 us (4%)
  local copies, waits for them, and re-layouts  3.68 us (1%)
  other arithmetic  3.62 us (1%)
    pallas_call x1, Pallas kernels, gather_all(): pl.pallas_call(functools.partial(gather_kernel, count, tiles_each), out_s...  208 us
    pallas_call x1, Pallas kernels, scene(): pl.pallas_call(functools.partial(scene_kernel, rows, rows * ring), out_sh...  17.8 us
    ppermute x2, waiting for transfers between devices, neighbours(): lax.ppermute(lax.slice_in_dim(block, 0, width, axis=dim), axes, backward)  17.5 us
    dot_general x1, matrix products, per_device(): jnp.einsum('tpf,fd->tpd', hidden, mlp_all, preferred_element_type=jnp.flo...  15.3 us
    all_to_all x1, waiting for transfers between devices, per_device(): split = lax.all_to_all(split, 'mp', split_axis=0, concat_axis=0, tiled=True)  8.76 us
    sub x1, matrix products, per_device(): soft_weights = jax.nn.softmax(scores, axis=-1).astype(jnp.bfloat16)  7.35 us
    dot_general x1, matrix products, per_device(): jnp.einsum('tpd,zkde->kztpe', normed, qkv_all, preferred_element_type=jnp...  6.74 us
  transfers between devices with their start and end apart: 6, of which 5 were waited for; matrix products, arithmetic and copies ran while one was open for 0% of the time, Pallas kernels for 0%

commit v1 on v0

--- a/solution.py
+++ b/solution.py
@@ -66,10 +66,14 @@
         )
     pl.semaphore_wait(barrier, 3 + count - 1)
 
+    shared = (True, True, False, False)
+
     def piece(which, origin, owner, part=None):
-        rows = gathered[which].shape[1] // PLANE
+        split = PLANE if shared[which] else PLANE // 2
+        rows = gathered[which].shape[1] // split
         cols = gathered[which].shape[2]
-        begin = pl.multiple_of(owner % PLANE * rows, rows)
+        place = owner % PLANE if shared[which] else owner % PLANE // 2
+        begin = pl.multiple_of(place * rows, rows)
         if part is None:
             return (origin, pl.ds(begin, rows))
         if rows % 32 == 0:
@@ -112,7 +116,16 @@
 
     def own_piece(which):
         rows = shards[which].shape[0] // PLANE
-        return shards[which].at[pl.ds(pl.multiple_of(me_t % PLANE * rows, rows), rows)]
+        place = me_t % PLANE
+        if not shared[which]:
+            place = place % 2 * (PLANE // 2) + place // 2
+        return shards[which].at[pl.ds(pl.multiple_of(place * rows, rows), rows)]
+
+    def own_part(which):
+        if shared[which]:
+            return shards[which]
+        rows = shards[which].shape[0] // 2
+        return shards[which].at[pl.ds(pl.multiple_of(me_t % 2 * rows, rows), rows)]
 
     def first_sends(which, wait):
         for up in (True, False):
@@ -180,23 +193,28 @@
                 chain(which, origin, gathered[which].at[piece(which, origin, me_t)], up).start()
         go(which, origin, 1)
         go(which, origin, 2)
-        go(which, origin, 5)
+        if shared[which]:
+            go(which, origin, 5)
 
     def stage_b(which, index):
         origin, _ = source(index)
         arrived(which, origin, 1)
         go(which, origin, 3)
-        go(which, origin, 6)
+        if shared[which]:
+            go(which, origin, 6)
         arrived(which, origin, 2)
         go(which, origin, 4)
-        go(which, origin, 7)
+        if shared[which]:
+            go(which, origin, 7)
 
     def stage_c(which, index):
         origin, _ = source(index)
         arrived(which, origin, 3)
-        go(which, origin, 8)
+        if shared[which]:
+            go(which, origin, 8)
         arrived(which, origin, 4)
-        go(which, origin, 9)
+        if shared[which]:
+            go(which, origin, 9)
 
     def stage_d(which, index):
         origin, _ = source(index)
@@ -204,7 +222,7 @@
             arrived(which, origin, kind)
 
     own_copies = [
-        pltpu.make_async_copy(shards[which], gathered[which].at[me_z], own_sem.at[which])
+        pltpu.make_async_copy(own_part(which), gathered[which].at[me_z], own_sem.at[which])
         for which in range(4)
     ]
     first_sends(0, False)
@@ -223,7 +241,8 @@
                     first_sends(units[at][0] + 2, False)
 
     for which, index in units:
-        stage_d(which, index)
+        if shared[which]:
+            stage_d(which, index)
     own_tokens.wait()
     for copy in token_copies:
         copy.wait()
@@ -240,7 +259,7 @@
                     chain(
                         which, origin, gathered[which].at[piece(which, origin, me_t)], up
                     ).wait_send()
-            for kind in range(1, KINDS):
+            for kind in range(1, KINDS if shared[which] else 5):
                 owner, part, bit = outward[kind]
                 ring(which, origin, owner, kind, part, bit).wait_send()
 
@@ -254,8 +273,8 @@
         out_shape=(
             jax.ShapeDtypeStruct((tiles_each, PATCHES, tokens.shape[2]), jnp.bfloat16),
         ) + tuple(
-            jax.ShapeDtypeStruct((count,) + part.shape, jnp.bfloat16)
-            for part in (qkv, out, into, mlp)
+            jax.ShapeDtypeStruct((count, part.shape[0] // cut, part.shape[1]), jnp.bfloat16)
+            for part, cut in ((qkv, 1), (out, 1), (into, 2), (mlp, 2))
         ),
         in_specs=[any_space] * 5,
         out_specs=(any_space,) * 5,
@@ -425,10 +444,21 @@
     context = context.astype(jnp.bfloat16).reshape(tiles_each, PATCHES, width)
     attention = jnp.einsum("tpe,ed->tpd", context, out_all, preferred_element_type=jnp.float32)
     middle = (seq.astype(jnp.float32) + attention).astype(jnp.bfloat16)
+    middle, guide_low, guide_high = lax.optimization_barrier((middle, guide_low, guide_high))
     normed_mid = layer_norm(middle, ln_gain_two)
-    hidden = jnp.einsum("tpd,fd->tpf", normed_mid, in_all, preferred_element_type=jnp.float32)
-    hidden = jax.nn.gelu(hidden).astype(jnp.bfloat16)
-    mlp_part = jnp.einsum("tpf,fd->tpd", hidden, mlp_all, preferred_element_type=jnp.float32)
+    swap = [(i, i + 1 - 2 * (i % 2)) for i in range(groups)]
+
+    def mlp_in(rows):
+        hidden = jnp.einsum("tpd,fd->tpf", rows, in_all, preferred_element_type=jnp.float32)
+        return jax.nn.gelu(hidden).astype(jnp.bfloat16)
+
+    def mlp_out(hidden):
+        return jnp.einsum("tpf,fd->tpd", hidden, mlp_all, preferred_element_type=jnp.float32)
+
+    beside = lax.ppermute(normed_mid, "tile", swap)
+    hidden, beside = lax.optimization_barrier((mlp_in(normed_mid), beside))
+    beside = lax.ppermute(mlp_out(mlp_in(beside)).astype(jnp.bfloat16), "tile", swap)
+    mlp_part = mlp_out(hidden) + beside.astype(jnp.float32)
     features = (middle.astype(jnp.float32) + mlp_part).astype(jnp.bfloat16)
     mask_here = lax.dynamic_slice_in_dim(
         land_mask, lax.axis_index("mp") * tiles_each, tiles_each, 0

time: 315 us -> 257 us (0.82)
  Pallas kernels: 226 us -> 163 us
  waiting for transfers between devices: 30.8 us -> 26.4 us
  starting transfers between devices: 13.9 us -> 17.2 us
  matrix products: 36.2 us -> 39.4 us
    pallas_call x1, Pallas kernels: 208 us -> 145 us  [gather_all(): pl.pallas_call(functools.partial(gather_kernel, count, tiles_each), out_s...]
    ppermute x2, waiting for transfers between devices: 17.5 us -> 6.74 us  [neighbours(): lax.ppermute(lax.slice_in_dim(block, 0, width, axis=dim), axes, backward)]
    dot_general x1, matrix products: 0.44 us -> 5.83 us  [per_device(): jnp.einsum('tpd,dc->tpc', features, proj_weight, preferred_element_type=j...]
    all_to_all x1, waiting for transfers between devices: 2.73 us -> 6.85 us  [per_device(): lax.all_to_all(outgoing, 'tile', split_axis=0, concat_axis=0, tiled=True)]
    dot_general x1 -> x2, matrix products: 15.3 us -> 13.1 us  [the longest x1 8.43 us: mlp_out(): jnp.einsum('tpf,fd->tpd', hidden, mlp_all, preferred_element_type=jnp.flo...]
  transfers between devices with their start and end apart: 6 -> 8, of which waited for: 5 -> 5; matrix products, arithmetic and copies ran while one was open for 0% -> 11% of each run, Pallas kernels for 0% -> 57%
where the time goes in v1:
time: 257 us
  Pallas kernels  163 us (63%)
  matrix products  39.4 us (15%)
  waiting for transfers between devices  26.4 us (10%)
  starting transfers between devices  17.2 us (7%)
  local copies, waits for them, and re-layouts  5.98 us (2%)
  other arithmetic  4.21 us (2%)
    pallas_call x1, Pallas kernels, gather_all(): pl.pallas_call(functools.partial(gather_kernel, count, tiles_each), out_s...  145 us
    pallas_call x1, Pallas kernels, scene(): pl.pallas_call(functools.partial(scene_kernel, rows, rows * ring), out_sh...  17.7 us
    all_to_all x1, waiting for transfers between devices, per_device(): split = lax.all_to_all(split, 'mp', split_axis=0, concat_axis=0, tiled=True)  9.54 us
    dot_general x1, matrix products, mlp_out(): jnp.einsum('tpf,fd->tpd', hidden, mlp_all, preferred_element_type=jnp.flo...  8.43 us
    sub x1, matrix products, per_device(): soft_weights = jax.nn.softmax(scores, axis=-1).astype(jnp.bfloat16)  7.32 us
    ppermute x2, starting transfers between devices, neighbours(): lax.ppermute(lax.slice_in_dim(block, block.shape[dim] - width, None, axis...  6.91 us
    all_to_all x1, waiting for transfers between devices, per_device(): lax.all_to_all(outgoing, 'tile', split_axis=0, concat_axis=0, tiled=True)  6.85 us
    dot_general x1, matrix products, per_device(): jnp.einsum('tpd,zkde->kztpe', normed, qkv_all, preferred_element_type=jnp...  6.74 us
  transfers between devices with their start and end apart: 8, of which 5 were waited for; matrix products, arithmetic and copies ran while one was open for 11% of the time, Pallas kernels for 57%

profile of v1, /device:TPU:0, one launch (start us, length us, event | category | flops | bytes accessed | tf_op | source)
XLA Modules:
  0.0 256.7 jit_solution(18187783604930293666)
XLA Ops:
  0.0 0.0 copy-start
  0.0 2.1 fusion.70
  2.1 4.9 %collective-permute-start = (bf16[3,256,256]{2,1,0:T(8,128)(2,1)}, bf16[3,256,256]{2,1,0:T(8,128)(2,1)S(1)}, u32[]{:S(2)}, u32[]{:S(2)}) collective-permute-start(bf16[3,256,256]{2,1,0:T(8,128)(2,1)} %get-tuple-element.31), channel_id=1, source_target_pairs={{0,1},{1,2},{2,3},{3,4},{4,5},{5,6},{6,7},{7,8},{8,9},{9,10},{10,1... | collective-permute-start | bytes 1179656 | tf_op jit(solution)/shard_map/ppermute | solution.py:299
  7.1 1.3 collective-permute-start.1
  8.4 0.0 copy-start.9
  8.4 145.4 %gather_weights.1 = (bf16[2,256,1024]{2,1,0:T(8,128)(2,1)}, bf16[4,3072,256]{2,1,0:T(8,128)(2,1)}, bf16[4,256,1024]{2,1,0:T(8,128)(2,1)}, bf16[4,512,1024]{2,1,0:T(8,128)(2,1)}, bf16[4,512,1024]{2,1,0:T(8,128)(2,1)}) custom-call(bf16[8,64,1024]{2,1,0:T(8,128)(2,1)} %tokens_ref.1, bf16[3072,256]{1,0:T(8,128)(2,1)} %bitcast.59, bf16[256,1024]{1,0:T(8,128)(2,1)} %out_ref.1, ...), custom_call_target="tpu_custom_call" | custom-call | tf_op jit(solution)/shard_map/gather_weights/pallas_call | solution.py:271
  153.8 1.4 convert_reduce_fusion.1
  155.3 1.6 fusion.30
  156.9 0.0 copy-done.9
  156.9 6.7 %convert_bitcast_fusion = bf16[3,4,2,256,256]{3,4,2,0,1:T(8,128)(2,1)S(1)} fusion(bf16[4,3,1024,256,1]{3,2,4,1,0:T(8,128)(2,1)} %bitcast.65, bf16[2,256,1024]{2,1,0:T(8,128)(2,1)} %get-tuple-element.15, f32[1024]{0:T(1024)S(1)} %copy-done.9, f32[2,256]{1,0:T(2,128)S(1)} %add_rsqrt_fusion.1, f32[2,256]{1,0:T(2,128)S(1)} %broadcast_multiply_fusion.1), kind=kOutput, calls=%fused_computation.29 | convolution fusion | flops 3225419776 | bytes 10493952 | tf_op jit(solution)/shard_map/tpd,zkde->kztpe/dot_general | solution.py:433
  163.7 1.2 fusion.69
  164.9 7.3 %fusion.72 = (f32[4,2,4,256]{3,2,1,0:T(4,128)S(1)}, f32[4,2,4,256,256]{3,4,2,1,0:T(8,128)}) fusion(bf16[4,2,256,4,64]{2,4,3,1,0:T(8,128)(2,1)} %bitcast.63, bf16[4,2,256,4,64]{2,4,3,1,0:T(8,128)(2,1)S(1)} %bitcast.62), kind=kOutput, calls=%fused_computation.96 | convolution fusion | flops 274727168 | bytes 10518528 | tf_op jit(solution)/shard_map/sub | solution.py:440
  172.2 0.0 copy-start.7
  172.2 4.4 %fusion.35 = bf16[2,4,4,64,256]{4,3,2,1,0:T(8,128)(2,1)S(1)} fusion(bf16[4,2,256,4,64]{2,4,3,1,0:T(8,128)(2,1)S(1)} %bitcast.61, f32[4,2,4,256,256]{3,4,2,1,0:T(8,128)} %get-tuple-element.35, f32[4,2,4,256]{3,2,1,0:T(4,128)S(1)} %get-tuple-element.34), kind=kOutput, calls=%fused_computation.45 | convolution fusion | flops 273154048 | bytes 10518528 | tf_op jit(solution)/shard_map/zthpq,ztqhe->tpzhe/dot_general | solution.py:441
  176.6 0.0 copy-done.3
  176.7 0.0 copy-start.4
  176.7 1.3 fusion.33
  177.9 0.0 collective-permute-done.guide_low
  178.0 0.0 collective-permute-done.1.guide_high
  178.0 0.2 convert_reduce_fusion
  178.2 0.4 fusion.27
  178.6 0.4 fusion.29
  179.0 0.1 collective-permute-start.2
  179.1 4.7 %fusion.11 = bf16[2,256,2048]{2,1,0:T(8,128)(2,1)} fusion(bf16[2,256,1024]{2,1,0:T(8,128)(2,1)S(1)} %fusion.29, bf16[2048,1024,1]{1,0,2:T(8,128)(2,1)S(1)} %bitcast.69), kind=kOutput, calls=%fused_computation.14 | convolution fusion | flops 2156920832 | bytes 7340032 | tf_op jit(solution)/shard_map/tpd,fd->tpf/dot_general | solution.py:452
  183.8 0.0 collective-permute-done.2
  183.8 1.0 copy-done.8
  184.8 8.4 %convolution_convert_fusion = bf16[2,256,1024]{2,1,0:T(8,128)(2,1)S(1)} fusion(bf16[2048,1024,1]{1,0,2:T(8,128)(2,1)} %bitcast.66, bf16[2,256,1024]{2,1,0:T(8,128)(2,1)} %copy-done.8, bf16[2048,1024,1]{1,0,2:T(8,128)(2,1)} %bitcast.68), kind=kOutput, calls=%fused_computation.46 | convolution fusion | flops 4304928768 | bytes 10485760 | tf_op jit(solution)/shard_map/tpf,fd->tpd/dot_general | solution.py:456
  193.2 0.6 collective-permute-start.3
  193.8 0.1 dynamic-slice_convert_fusion
  193.9 2.3 collective-permute-done.3
  196.2 0.0 copy-done
  196.2 5.8 %fusion.38 = bf16[2,256,256]{2,1,0:T(8,128)(2,1)S(1)} fusion(bf16[2,256,1024]{2,1,0:T(8,128)(2,1)S(1)} %fusion.33, bf16[2,256,1024]{2,1,0:T(8,128)(2,1)} %collective-permute-done.3, bf16[2,256,2048]{2,1,0:T(8,128)(2,1)} %fusion.11, bf16[2048,1024,1]{1,0,2:T(8,128)(2,1)} %bitcast.67, bf16[1024,256]{1,0:T(8,128)(2,1)S(1)} %copy-done, ...), kind=kOutput, calls=%fused_computation.49 | convolution fusion | flops 2419195904 | bytes 9175044 | tf_op jit(solution)/shard_map/tpd,dc->tpc/dot_general | solution.py:466
  202.0 0.0 copy-start.1
  202.0 0.0 copy-start.2
  202.1 0.7 copy.54
  202.8 3.4 %all-to-all-start = ((bf16[4,2,64,256]{3,2,1,0:T(8,128)(2,1)}), bf16[4,2,64,256]{3,2,1,0:T(8,128)(2,1)S(1)}, u32[]{:S(2)}, u32[]{:S(2)}) async-start(bf16[4,2,64,256]{3,2,1,0:T(8,128)(2,1)} %bitcast.57), calls=%async_computation | async-start | bytes 524288 | tf_op jit(solution)/shard_map/all_to_all | solution.py:471
  206.2 0.1 dynamic_slice.6
  206.3 9.5 %all-to-all-done = bf16[4,2,64,256]{3,2,1,0:T(8,128)(2,1)S(1)} async-done(((bf16[4,2,64,256]{3,2,1,0:T(8,128)(2,1)}), bf16[4,2,64,256]{3,2,1,0:T(8,128)(2,1)S(1)}, u32[]{:S(2)}, u32[]{:S(2)}) %all-to-all-start) | async-done | bytes 262176 | tf_op jit(solution)/shard_map/all_to_all | solution.py:471
  215.8 0.2 convolution_convert_fusion.1
  216.1 0.8 copy.31
  216.9 3.4 %all-to-all-start.1 = ((bf16[8,64,256]{2,1,0:T(8,128)(2,1)}), bf16[8,64,256]{2,1,0:T(8,128)(2,1)S(1)}, u32[]{:S(2)}, u32[]{:S(2)}) async-start(bf16[8,64,256]{2,1,0:T(8,128)(2,1)} %copy.31), calls=%async_computation.1 | async-start | bytes 524288 | tf_op jit(solution)/shard_map/all_to_all | solution.py:493
  220.3 6.9 %all-to-all-done.1 = bf16[8,64,256]{2,1,0:T(8,128)(2,1)S(1)} async-done(((bf16[8,64,256]{2,1,0:T(8,128)(2,1)}), bf16[8,64,256]{2,1,0:T(8,128)(2,1)S(1)}, u32[]{:S(2)}, u32[]{:S(2)}) %all-to-all-start.1) | async-done | bytes 262176 | tf_op jit(solution)/shard_map/all_to_all | solution.py:493
  227.1 0.5 fusion.48
  227.7 2.0 collective-permute-start.4
  229.7 1.5 collective-permute-start.5
  231.2 1.0 collective-permute-done.4.low_ref
  232.2 6.7 %collective-permute-done.5.high_ref = bf16[8,32,256]{2,1,0:T(8,128)(2,1)S(1)} collective-permute-done((bf16[8,32,256]{2,1,0:T(8,128)(2,1)S(1)}, bf16[8,32,256]{2,1,0:T(8,128)(2,1)S(1)}, u32[]{:S(2)}, u32[]{:S(2)}) %collective-permute-start.5) | collective-permute-done | bytes 131104 | tf_op jit(solution)/shard_map/ppermute | solution.py:300
  238.9 17.7 %scene_convolutions.1 = bf16[8,256,256]{2,1,0:T(8,128)(2,1)} custom-call(bf16[8,32,256]{2,1,0:T(8,128)(2,1)S(1)} %collective-permute-done.4.low_ref, bf16[8,64,256]{2,1,0:T(8,128)(2,1)S(1)} %copy.53.mid_ref, bf16[8,32,256]{2,1,0:T(8,128)(2,1)S(1)} %collective-permute-done.5.high_ref, bf16[3,256,256]{2,1,0:T(8,128)(2,1)S(1)} %collective-permute-done.guide_low, ...), custom_call_target="tpu_custom_call" | custom-call | tf_op jit(solution)/shard_map/scene_convolutions/pallas_call | solution.py:388
  (20 shorter events, 0.1 us)
Async XLA Ops:
  0.0 196.2 %copy-start = (bf16[1024,256]{1,0:T(8,128)(2,1)S(1)}, bf16[1024,256]{1,0:T(8,128)(2,1)}, u32[]{:S(2)}) copy-start(bf16[1024,256]{1,0:T(8,128)(2,1)} %param.20) | copy-start | bytes 1572868
  2.1 175.8 %collective-permute-start = (bf16[3,256,256]{2,1,0:T(8,128)(2,1)}, bf16[3,256,256]{2,1,0:T(8,128)(2,1)S(1)}, u32[]{:S(2)}, u32[]{:S(2)}) collective-permute-start(bf16[3,256,256]{2,1,0:T(8,128)(2,1)} %get-tuple-element.31), channel_id=1, source_target_pairs={{0,1},{1,2},{2,3},{3,4},{4,5},{5,6},{6,7},{7,8},{8,9},{9,10},{10,1... | collective-permute-start | bytes 1179656 | tf_op jit(solution)/shard_map/ppermute | solution.py:299
  7.1 170.9 %collective-permute-start.1 = (bf16[3,256,256]{2,1,0:T(8,128)(2,1)}, bf16[3,256,256]{2,1,0:T(8,128)(2,1)S(1)}, u32[]{:S(2)}, u32[]{:S(2)}) collective-permute-start(bf16[3,256,256]{2,1,0:T(8,128)(2,1)} %get-tuple-element.30), channel_id=1, source_target_pairs={{1,0},{2,1},{3,2},{4,3},{5,4},{6,5},{7,6},{8,7},{9,8},{10,9},{11,1... | collective-permute-start | bytes 1179656 | tf_op jit(solution)/shard_map/ppermute | solution.py:300
  8.4 148.6 %copy-start.9 = (f32[1024]{0:T(1024)S(1)}, f32[1024]{0:T(1024)}, u32[]{:S(2)}) copy-start(f32[1024]{0:T(1024)} %param.14) | copy-start | bytes 12292
  172.2 4.4 %copy-start.3 = (bf16[2,256,1024]{2,1,0:T(8,128)(2,1)S(1)}, bf16[2,256,1024]{2,1,0:T(8,128)(2,1)}, u32[]{:S(2)}) copy-start(bf16[2,256,1024]{2,1,0:T(8,128)(2,1)} %get-tuple-element.15) | copy-start | bytes 3145732
  172.2 4.4 %copy-start.7 = (bf16[4,256,1024]{2,1,0:T(8,128)(2,1)S(1)}, bf16[4,256,1024]{2,1,0:T(8,128)(2,1)}, u32[]{:S(2)}) copy-start(bf16[4,256,1024]{2,1,0:T(8,128)(2,1)} %get-tuple-element.17) | copy-start | bytes 6291460
  176.7 2.0 copy-start.4
  176.7 2.4 copy-start.6
  179.0 4.8 %collective-permute-start.2 = (bf16[2,256,1024]{2,1,0:T(8,128)(2,1)S(1)}, bf16[2,256,1024]{2,1,0:T(8,128)(2,1)S(1)}, u32[]{:S(2)}, u32[]{:S(2)}) collective-permute-start(bf16[2,256,1024]{2,1,0:T(8,128)(2,1)S(1)} %fusion.29), channel_id=1, source_target_pairs={{0,4},{4,0},{8,12},{12,8},{16,20},{20,16},{24,28},{28,24},{1,5},{5... | collective-permute-start | bytes 3145736 | tf_op jit(solution)/shard_map/ppermute | solution.py:458
  183.8 1.0 copy-start.8
  184.8 9.0 %copy-start.10 = (s32[8]{0:T(128)S(1)}, s32[8]{0:T(128)}, u32[]{:S(2)}) copy-start(s32[8]{0:T(128)} %param.21) | copy-start | bytes 100
  193.2 3.0 %collective-permute-start.3 = (bf16[2,256,1024]{2,1,0:T(8,128)(2,1)S(1)}, bf16[2,256,1024]{2,1,0:T(8,128)(2,1)}, u32[]{:S(2)}, u32[]{:S(2)}) collective-permute-start(bf16[2,256,1024]{2,1,0:T(8,128)(2,1)S(1)} %convolution_convert_fusion), channel_id=1, source_target_pairs={{0,4},{4,0},{8,12},{12,8},{16,20},{20,16},{24,28},{28,24},{1,5},{5... | collective-permute-start | bytes 3145736 | tf_op jit(solution)/shard_map/ppermute | solution.py:460
  193.8 12.3 %copy-start.5 = (s32[64]{0:T(128)S(1)}, s32[64]{0:T(128)}, u32[]{:S(2)}) copy-start(s32[64]{0:T(128)} %param.22) | copy-start | bytes 772
  202.0 36.9 %copy-start.1 = (bf16[8,256,256]{2,1,0:T(8,128)(2,1)S(1)}, bf16[8,256,256]{2,1,0:T(8,128)(2,1)}, u32[]{:S(2)}) copy-start(bf16[8,256,256]{2,1,0:T(8,128)(2,1)} %guide_mid.1) | copy-start | bytes 3145732
  202.0 36.9 %copy-start.2 = (f32[3,256]{1,0:T(4,128)S(1)}, f32[3,256]{1,0:T(4,128)}, u32[]{:S(2)}) copy-start(f32[3,256]{1,0:T(4,128)} %bias_ref.1) | copy-start | bytes 9220
  202.8 13.1 %all-to-all-start = ((bf16[4,2,64,256]{3,2,1,0:T(8,128)(2,1)}), bf16[4,2,64,256]{3,2,1,0:T(8,128)(2,1)S(1)}, u32[]{:S(2)}, u32[]{:S(2)}) async-start(bf16[4,2,64,256]{3,2,1,0:T(8,128)(2,1)} %bitcast.57), calls=%async_computation | async-start | bytes 524288 | tf_op jit(solution)/shard_map/all_to_all | solution.py:471
  216.9 10.3 %all-to-all-start.1 = ((bf16[8,64,256]{2,1,0:T(8,128)(2,1)}), bf16[8,64,256]{2,1,0:T(8,128)(2,1)S(1)}, u32[]{:S(2)}, u32[]{:S(2)}) async-start(bf16[8,64,256]{2,1,0:T(8,128)(2,1)} %copy.31), calls=%async_computation.1 | async-start | bytes 524288 | tf_op jit(solution)/shard_map/all_to_all | solution.py:493
  227.7 4.5 %collective-permute-start.4 = (bf16[8,32,256]{2,1,0:T(8,128)(2,1)S(1)}, bf16[8,32,256]{2,1,0:T(8,128)(2,1)S(1)}, u32[]{:S(2)}, u32[]{:S(2)}) collective-permute-start(bf16[8,32,256]{2,1,0:T(8,128)(2,1)S(1)} %get-tuple-element.33), channel_id=1, source_target_pairs={{0,1},{1,2},{2,3},{3,4},{4,5},{5,6},{6,7},{7,8},{8,9},{9,10},{10,1... | collective-permute-start | bytes 393224 | tf_op jit(solution)/shard_map/ppermute | solution.py:299
  229.7 9.2 %collective-permute-start.5 = (bf16[8,32,256]{2,1,0:T(8,128)(2,1)S(1)}, bf16[8,32,256]{2,1,0:T(8,128)(2,1)S(1)}, u32[]{:S(2)}, u32[]{:S(2)}) collective-permute-start(bf16[8,32,256]{2,1,0:T(8,128)(2,1)S(1)} %get-tuple-element.32), channel_id=1, source_target_pairs={{1,0},{2,1},{3,2},{4,3},{5,4},{6,5},{7,6},{8,7},{9,8},{10,9},{11,1... | collective-permute-start | bytes 393224 | tf_op jit(solution)/shard_map/ppermute | solution.py:300

commit v2 on v1

--- a/solution.py
+++ b/solution.py
@@ -12,8 +12,8 @@
 UP = 2
 PATCHES = 256
 HALO = 3
-PLANE = 8
-KINDS = 10
+SPREAD = 4
+KINDS = 5
 
 
 def layer_norm(values, gain):
@@ -54,7 +54,7 @@
     gathered = (qkv_all, out_all, in_all, mlp_all)
 
     barrier = pltpu.get_barrier_semaphore()
-    for bit in (1, 2, 4):
+    for bit in (2, 4):
         pl.semaphore_signal(
             barrier, inc=1, device_id={"tile": flip(me_t, bit), "mp": me_z},
             device_id_type=pl.DeviceIdType.MESH,
@@ -64,16 +64,12 @@
             barrier, inc=1, device_id={"tile": me_t, "mp": lax.rem(me_z + step, count)},
             device_id_type=pl.DeviceIdType.MESH,
         )
-    pl.semaphore_wait(barrier, 3 + count - 1)
-
-    shared = (True, True, False, False)
+    pl.semaphore_wait(barrier, 2 + count - 1)
 
     def piece(which, origin, owner, part=None):
-        split = PLANE if shared[which] else PLANE // 2
-        rows = gathered[which].shape[1] // split
+        rows = gathered[which].shape[1] // SPREAD
         cols = gathered[which].shape[2]
-        place = owner % PLANE if shared[which] else owner % PLANE // 2
-        begin = pl.multiple_of(place * rows, rows)
+        begin = pl.multiple_of(owner // 2 % SPREAD * rows, rows)
         if part is None:
             return (origin, pl.ds(begin, rows))
         if rows % 32 == 0:
@@ -105,37 +101,28 @@
     )
     own_tokens.start()
 
-    def chain(which, origin, src, up):
-        slot = 1 if up else 0
-        target = me_z + 1 if up else me_z - 1
-        ref = src
-        return remote(
-            ref, gathered[which].at[piece(which, origin, me_t)],
-            chain_send.at[which, origin, slot], recv_sem.at[which, origin, 0], me_t, target,
-        )
-
-    def own_piece(which):
-        rows = shards[which].shape[0] // PLANE
-        place = me_t % PLANE
-        if not shared[which]:
-            place = place % 2 * (PLANE // 2) + place // 2
-        return shards[which].at[pl.ds(pl.multiple_of(place * rows, rows), rows)]
-
     def own_part(which):
-        if shared[which]:
+        if which == 0:
             return shards[which]
         rows = shards[which].shape[0] // 2
         return shards[which].at[pl.ds(pl.multiple_of(me_t % 2 * rows, rows), rows)]
 
-    def first_sends(which, wait):
-        for up in (True, False):
-            @pl.when(me_z + 1 < count if up else me_z > 0)
-            def _():
-                copy = chain(which, me_z, own_piece(which), up)
-                if wait:
-                    copy.wait_send()
-                else:
-                    copy.start()
+    def own_piece(which):
+        rows = gathered[which].shape[1] // SPREAD
+        base = 0 if which == 0 else me_t % 2 * SPREAD
+        place = base + me_t // 2 % SPREAD
+        return shards[which].at[pl.ds(pl.multiple_of(place * rows, rows), rows)]
+
+    def along(which, step):
+        return remote(
+            own_piece(which), gathered[which].at[piece(which, me_z, me_t)],
+            chain_send.at[which, step], recv_sem.at[which, me_z, 0],
+            me_t, lax.rem(me_z + step, count),
+        )
+
+    def first_sends(which):
+        for step in range(1, count):
+            along(which, step).start()
 
     def source(index):
         below, above = me_z, count - 1 - me_z
@@ -143,7 +130,7 @@
         paired = index < 2 * least
         down_side = jnp.where(paired, index % 2 == 0, below > above)
         far = jnp.where(paired, index // 2 + 1, index - least + 1)
-        return jnp.where(down_side, me_z - far, me_z + far), down_side
+        return jnp.where(down_side, me_z - far, me_z + far)
 
     def ring(which, origin, owner, kind, part, bit):
         where = piece(which, origin, owner, part)
@@ -153,82 +140,52 @@
             flip(me_t, bit), me_z,
         )
 
-    def routes(device):
-        first_bit = 2 + 2 * (device % 2)
-        second_bit = 4 - 2 * (device % 2)
-        first_of, second_of = flip(device, first_bit), flip(device, second_bit)
-        both = flip(flip(device, 2), 4)
-        return {
-            1: (device, None, first_bit),
-            2: (device, None, second_bit),
-            3: (first_of, 0, second_bit),
-            4: (second_of, 1, first_bit),
-            5: (device, None, 1),
-            6: (first_of, None, 1),
-            7: (second_of, None, 1),
-            8: (both, 0, 1),
-            9: (both, 1, 1),
-        }
-
-    outward = routes(me_t)
-    inward = routes(flip(me_t, 1))
+    first_bit = 2 + 2 * (me_t % 2)
+    second_bit = 4 - 2 * (me_t % 2)
+    outward = {
+        1: (me_t, None, first_bit),
+        2: (me_t, None, second_bit),
+        3: (flip(me_t, first_bit), 0, second_bit),
+        4: (flip(me_t, second_bit), 1, first_bit),
+    }
 
     def go(which, origin, kind):
         owner, part, bit = outward[kind]
         ring(which, origin, owner, kind, part, bit).start()
 
     def arrived(which, origin, kind):
-        owner, part, bit = (outward if kind < 5 else inward)[kind]
-        if kind < 5:
-            owner = flip(owner, bit)
-        ring(which, origin, owner, kind, part, bit).wait_recv()
+        owner, part, bit = outward[kind]
+        ring(which, origin, flip(owner, bit), kind, part, bit).wait_recv()
 
     def stage_a(which, index):
-        origin, down_side = source(index)
-        chain(which, origin, gathered[which].at[piece(which, origin, me_t)], True).wait_recv()
-        for up in (True, False):
-            @pl.when((down_side & (me_z + 1 < count)) if up else
-                     (jnp.logical_not(down_side) & (me_z > 0)))
-            def _():
-                chain(which, origin, gathered[which].at[piece(which, origin, me_t)], up).start()
+        origin = source(index)
+        where = gathered[which].at[piece(which, origin, me_t)]
+        remote(
+            where, where, chain_send.at[which, 0], recv_sem.at[which, origin, 0], me_t, origin
+        ).wait_recv()
         go(which, origin, 1)
         go(which, origin, 2)
-        if shared[which]:
-            go(which, origin, 5)
 
     def stage_b(which, index):
-        origin, _ = source(index)
+        origin = source(index)
         arrived(which, origin, 1)
         go(which, origin, 3)
-        if shared[which]:
-            go(which, origin, 6)
         arrived(which, origin, 2)
         go(which, origin, 4)
-        if shared[which]:
-            go(which, origin, 7)
 
     def stage_c(which, index):
-        origin, _ = source(index)
+        origin = source(index)
         arrived(which, origin, 3)
-        if shared[which]:
-            go(which, origin, 8)
         arrived(which, origin, 4)
-        if shared[which]:
-            go(which, origin, 9)
-
-    def stage_d(which, index):
-        origin, _ = source(index)
-        for kind in (5, 6, 7, 8, 9):
-            arrived(which, origin, kind)
 
     own_copies = [
         pltpu.make_async_copy(own_part(which), gathered[which].at[me_z], own_sem.at[which])
         for which in range(4)
     ]
-    first_sends(0, False)
+    first_sends(0)
     for copy in own_copies:
         copy.start()
-    first_sends(1, False)
+    first_sends(1)
 
     units = [(which, index) for which in range(4) for index in range(count - 1)]
     stages = (stage_a, stage_b, stage_c)
@@ -238,28 +195,19 @@
             if 0 <= at < len(units):
                 stage(*units[at])
                 if late == 0 and units[at][1] == 0 and units[at][0] + 2 < 4:
-                    first_sends(units[at][0] + 2, False)
-
-    for which, index in units:
-        if shared[which]:
-            stage_d(which, index)
+                    first_sends(units[at][0] + 2)
+
     own_tokens.wait()
     for copy in token_copies:
         copy.wait()
     for copy in own_copies:
         copy.wait()
     for which in range(4):
-        first_sends(which, True)
+        for step in range(1, count):
+            along(which, step).wait_send()
         for index in range(count - 1):
-            origin, down_side = source(index)
-            for up in (True, False):
-                @pl.when((down_side & (me_z + 1 < count)) if up else
-                         (jnp.logical_not(down_side) & (me_z > 0)))
-                def _():
-                    chain(
-                        which, origin, gathered[which].at[piece(which, origin, me_t)], up
-                    ).wait_send()
-            for kind in range(1, KINDS if shared[which] else 5):
+            origin = source(index)
+            for kind in range(1, KINDS):
                 owner, part, bit = outward[kind]
                 ring(which, origin, owner, kind, part, bit).wait_send()
 
@@ -274,7 +222,7 @@
             jax.ShapeDtypeStruct((tiles_each, PATCHES, tokens.shape[2]), jnp.bfloat16),
         ) + tuple(
             jax.ShapeDtypeStruct((count, part.shape[0] // cut, part.shape[1]), jnp.bfloat16)
-            for part, cut in ((qkv, 1), (out, 1), (into, 2), (mlp, 2))
+            for part, cut in ((qkv, 1), (out, 2), (into, 2), (mlp, 2))
         ),
         in_specs=[any_space] * 5,
         out_specs=(any_space,) * 5,
@@ -282,7 +230,7 @@
             pltpu.SemaphoreType.DMA((count,)),
             pltpu.SemaphoreType.DMA((count,)),
             pltpu.SemaphoreType.DMA((4,)),
-            pltpu.SemaphoreType.DMA((4, count, 2)),
+            pltpu.SemaphoreType.DMA((4, count)),
             pltpu.SemaphoreType.DMA((4, count, KINDS)),
             pltpu.SemaphoreType.DMA((4, count, KINDS)),
         ],
@@ -420,33 +368,44 @@
     tiles_each = tiles_here // parts
     guide_low, guide_high = neighbours(guide, HALO)
 
-    heads_local = qkv_weight.shape[2] // HEAD
+    swap = [(i, i + 1 - 2 * (i % 2)) for i in range(groups)]
+    heads_local = qkv_weight.shape[2] // HEAD // 2
+    half = lax.dynamic_slice_in_dim(
+        qkv_weight, lax.axis_index("tile") % 2 * (heads_local * HEAD), heads_local * HEAD, 2
+    )
     seq, qkv_all, out_all, in_all, mlp_all = gather_all(
-        tokens, qkv_weight.reshape(-1, qkv_weight.shape[2]), out_weight, in_weight, mlp_out_weight
+        tokens, half.reshape(-1, half.shape[2]), out_weight, in_weight, mlp_out_weight
     )
     qkv_all = qkv_all.reshape(parts, 3, width, heads_local * HEAD)
     out_all = out_all.reshape(-1, width)
     in_all = in_all.reshape(-1, width)
     mlp_all = mlp_all.reshape(-1, width)
 
+    def project(rows):
+        return jnp.einsum(
+            "tpd,zkde->kztpe", rows, qkv_all, preferred_element_type=jnp.float32
+        ).astype(jnp.bfloat16)
+
+    def attend(projected):
+        shaped = projected.reshape(3, parts, tiles_each, PATCHES, heads_local, HEAD)
+        scores = jnp.einsum(
+            "ztphe,ztqhe->zthpq", shaped[0], shaped[1], preferred_element_type=jnp.float32
+        ) * HEAD ** (-0.5)
+        soft_weights = jax.nn.softmax(scores, axis=-1).astype(jnp.bfloat16)
+        context = jnp.einsum(
+            "zthpq,ztqhe->tpzhe", soft_weights, shaped[2], preferred_element_type=jnp.float32
+        )
+        context = context.astype(jnp.bfloat16).reshape(tiles_each, PATCHES, out_all.shape[0])
+        return jnp.einsum("tpe,ed->tpd", context, out_all, preferred_element_type=jnp.float32)
+
     normed = layer_norm(seq, ln_gain_one)
-    projected = jnp.einsum(
-        "tpd,zkde->kztpe", normed, qkv_all, preferred_element_type=jnp.float32
-    ).astype(jnp.bfloat16)
-    shaped = projected.reshape(3, parts, tiles_each, PATCHES, heads_local, HEAD)
-    scores = jnp.einsum(
-        "ztphe,ztqhe->zthpq", shaped[0], shaped[1], preferred_element_type=jnp.float32
-    ) * HEAD ** (-0.5)
-    soft_weights = jax.nn.softmax(scores, axis=-1).astype(jnp.bfloat16)
-    context = jnp.einsum(
-        "zthpq,ztqhe->tpzhe", soft_weights, shaped[2], preferred_element_type=jnp.float32
-    )
-    context = context.astype(jnp.bfloat16).reshape(tiles_each, PATCHES, width)
-    attention = jnp.einsum("tpe,ed->tpd", context, out_all, preferred_element_type=jnp.float32)
+    beside = lax.ppermute(normed, "tile", swap)
+    projected, beside = lax.optimization_barrier((project(normed), beside))
+    beside = lax.ppermute(attend(project(beside)).astype(jnp.bfloat16), "tile", swap)
+    attention = attend(projected) + beside.astype(jnp.float32)
     middle = (seq.astype(jnp.float32) + attention).astype(jnp.bfloat16)
     middle, guide_low, guide_high = lax.optimization_barrier((middle, guide_low, guide_high))
     normed_mid = layer_norm(middle, ln_gain_two)
-    swap = [(i, i + 1 - 2 * (i % 2)) for i in range(groups)]
 
     def mlp_in(rows):
         hidden = jnp.einsum("tpd,fd->tpf", rows, in_all, preferred_element_type=jnp.float32)

time: 257 us -> 266 us (1.035)
  Pallas kernels: 163 us -> 150 us
  matrix products: 39.4 us -> 48.6 us
  starting transfers between devices: 17.2 us -> 22.1 us
  local copies, waits for them, and re-layouts: 5.98 us -> 10.6 us
    pallas_call x1, Pallas kernels: 145 us -> 133 us  [gather_all(): pl.pallas_call(functools.partial(gather_kernel, count, tiles_each), out_s...]
    dot_general x3 -> x6, matrix products: 12.4 us -> 14.7 us  [the longest x2 5.9 us: attend(): jnp.einsum('zthpq,ztqhe->tpzhe', soft_weights, shaped[2], preferred_eleme...]
    sub x1 -> x2, matrix products: 7.32 us -> 9.36 us  [attend(): soft_weights = jax.nn.softmax(scores, axis=-1).astype(jnp.bfloat16)]
  transfers between devices with their start and end apart: 8 -> 10, of which waited for: 5 -> 5; matrix products, arithmetic and copies ran while one was open for 11% -> 12% of each run, Pallas kernels for 57% -> 0%
where the time goes in v2:
time: 266 us; the launch traced here: 265 us
  Pallas kernels  150 us (56%)
  matrix products  48.6 us (18%)
  waiting for transfers between devices  27.2 us (10%)
  starting transfers between devices  22.1 us (8%)
  local copies, waits for them, and re-layouts  10.6 us (4%)
  other arithmetic  5.95 us (2%)
    pallas_call x1, Pallas kernels, gather_all(): pl.pallas_call(functools.partial(gather_kernel, count, tiles_each), out_s...  133 us
    pallas_call x1, Pallas kernels, scene(): pl.pallas_call(functools.partial(scene_kernel, rows, rows * ring), out_sh...  17.7 us
    all_to_all x1, waiting for transfers between devices, per_device(): split = lax.all_to_all(split, 'mp', split_axis=0, concat_axis=0, tiled=True)  9.63 us
    dot_general x1, matrix products, mlp_out(): jnp.einsum('tpf,fd->tpd', hidden, mlp_all, preferred_element_type=jnp.flo...  9.42 us
    sub x2, matrix products, attend(): soft_weights = jax.nn.softmax(scores, axis=-1).astype(jnp.bfloat16)  9.36 us
    ppermute x2, starting transfers between devices, neighbours(): lax.ppermute(lax.slice_in_dim(block, block.shape[dim] - width, None, axis...  8.67 us
    all_to_all x1, waiting for transfers between devices, per_device(): lax.all_to_all(outgoing, 'tile', split_axis=0, concat_axis=0, tiled=True)  7.03 us
    dot_general x1, matrix products, per_device(): jnp.einsum('tpd,dc->tpc', features, proj_weight, preferred_element_type=j...  6.97 us
  transfers between devices with their start and end apart: 10, of which 5 were waited for; matrix products, arithmetic and copies ran while one was open for 12% of the time, Pallas kernels for 0%

profile of v2, /device:TPU:0, one launch (start us, length us, event | category | flops | bytes accessed | tf_op | source)
XLA Modules:
  0.0 265.1 jit_solution(14682691312302534448)
XLA Ops:
  0.0 1.4 copy-done
  1.4 1.0 constant_dynamic-slice_fusion
  2.4 132.6 %gather_weights.1 = (bf16[2,256,1024]{2,1,0:T(8,128)(2,1)}, bf16[4,3072,128]{2,1,0:T(8,128)(2,1)}, bf16[4,128,1024]{2,1,0:T(8,128)(2,1)}, bf16[4,512,1024]{2,1,0:T(8,128)(2,1)}, bf16[4,512,1024]{2,1,0:T(8,128)(2,1)}) custom-call(bf16[8,64,1024]{2,1,0:T(8,128)(2,1)} %tokens_ref.1, bf16[3072,128]{1,0:T(8,128)(2,1)} %bitcast.80, bf16[256,1024]{1,0:T(8,128)(2,1)} %out_ref.1, ...), custom_call_target="tpu_custom_call" | custom-call | tf_op jit(solution)/shard_map/gather_weights/pallas_call | solution.py:219
  135.1 1.6 convert_reduce_fusion.1
  136.7 1.6 fusion.31
  138.3 1.6 fusion.33
  139.9 0.1 collective-permute-start
  140.0 1.0 fusion.84
  141.0 6.7 %collective-permute-start.2 = (bf16[3,256,256]{2,1,0:T(8,128)(2,1)}, bf16[3,256,256]{2,1,0:T(8,128)(2,1)S(1)}, u32[]{:S(2)}, u32[]{:S(2)}) collective-permute-start(bf16[3,256,256]{2,1,0:T(8,128)(2,1)} %get-tuple-element.38), channel_id=1, source_target_pairs={{0,1},{1,2},{2,3},{3,4},{4,5},{5,6},{6,7},{7,8},{8,9},{9,10},{10,1... | collective-permute-start | bytes 1179656 | tf_op jit(solution)/shard_map/ppermute | solution.py:247
  147.7 1.5 collective-permute-start.3
  149.2 3.0 %fusion.42 = bf16[3,4,2,256,128]{3,4,2,0,1:T(8,128)(2,1)} fusion(bf16[4,3,1024,128,1]{3,2,4,1,0:T(8,128)(2,1)S(1)} %bitcast.93, bf16[2,256,1024]{2,1,0:T(8,128)(2,1)S(1)} %fusion.33), kind=kOutput, calls=%fused_computation.54 | convolution fusion | flops 1611399168 | bytes 5767168 | tf_op jit(solution)/shard_map/tpd,zkde->kztpe/dot_general | solution.py:385
  152.2 1.9 fusion.43
  154.1 1.2 fusion.82
  155.3 4.7 %fusion.87 = (f32[4,2,2,256]{3,2,1,0:T(2,128)S(1)}, f32[4,2,2,256,256]{3,4,2,1,0:T(8,128)}) fusion(bf16[4,2,256,2,64]{2,4,3,1,0:T(8,128)(2,1)} %bitcast.85, bf16[4,2,256,2,64]{2,4,3,1,0:T(8,128)(2,1)} %bitcast.84), kind=kOutput, calls=%fused_computation.113 | convolution fusion | flops 137363712 | bytes 5259264 | tf_op jit(solution)/shard_map/sub | solution.py:394
  160.0 2.9 %fusion.47 = bf16[2,4,2,64,256]{4,3,2,1,0:T(8,128)(2,1)S(1)} fusion(bf16[4,2,256,2,64]{2,4,3,1,0:T(8,128)(2,1)} %bitcast.82, f32[4,2,2,256,256]{3,4,2,1,0:T(8,128)} %get-tuple-element.44, f32[4,2,2,256]{3,2,1,0:T(2,128)S(1)} %get-tuple-element.43), kind=kOutput, calls=%fused_computation.59 | convolution fusion | flops 136577024 | bytes 5259264 | tf_op jit(solution)/shard_map/zthpq,ztqhe->tpzhe/dot_general | solution.py:395
  162.9 1.7 convolution_convert_fusion.2
  164.6 1.9 collective-permute-start.1
  166.6 1.2 fusion.83
  167.8 4.7 %fusion.86 = (f32[4,2,2,256]{3,2,1,0:T(2,128)S(1)}, f32[4,2,2,256,256]{3,4,2,1,0:T(8,128)}) fusion(bf16[4,2,256,2,64]{2,4,3,1,0:T(8,128)(2,1)} %bitcast.87, bf16[4,2,256,2,64]{2,4,3,1,0:T(8,128)(2,1)} %bitcast.86), kind=kOutput, calls=%fused_computation.112 | convolution fusion | flops 137363712 | bytes 5259264 | tf_op jit(solution)/shard_map/sub | solution.py:394
  172.4 3.0 %fusion.44 = bf16[2,4,2,64,256]{4,3,2,1,0:T(8,128)(2,1)S(1)} fusion(bf16[4,2,256,2,64]{2,4,3,1,0:T(8,128)(2,1)} %bitcast.83, f32[4,2,2,256,256]{3,4,2,1,0:T(8,128)} %get-tuple-element.42, f32[4,2,2,256]{3,2,1,0:T(2,128)S(1)} %get-tuple-element.41), kind=kOutput, calls=%fused_computation.58 | convolution fusion | flops 136577024 | bytes 5259264 | tf_op jit(solution)/shard_map/zthpq,ztqhe->tpzhe/dot_general | solution.py:395
  175.5 2.2 fusion.34
  177.7 0.2 convert_reduce_fusion
  178.0 0.4 fusion.28
  178.4 0.3 copy-done.4
  178.7 0.4 fusion.30
  179.1 0.1 collective-permute-start.4
  179.2 4.8 %fusion.9 = bf16[2,256,2048]{2,1,0:T(8,128)(2,1)} fusion(bf16[2,256,1024]{2,1,0:T(8,128)(2,1)S(1)} %fusion.30, bf16[2048,1024,1]{1,0,2:T(8,128)(2,1)S(1)} %bitcast.92), kind=kOutput, calls=%fused_computation.11 | convolution fusion | flops 2156920832 | bytes 7340032 | tf_op jit(solution)/shard_map/tpd,fd->tpf/dot_general | solution.py:411
  184.0 1.0 copy-done.13
  184.9 9.4 %convolution_convert_fusion.3 = bf16[2,256,1024]{2,1,0:T(8,128)(2,1)} fusion(bf16[2048,1024,1]{1,0,2:T(8,128)(2,1)} %bitcast.89, bf16[2,256,1024]{2,1,0:T(8,128)(2,1)} %copy-done.13, bf16[2048,1024,1]{1,0,2:T(8,128)(2,1)} %bitcast.91), kind=kOutput, calls=%fused_computation.57 | convolution fusion | flops 4304928768 | bytes 10485760 | tf_op jit(solution)/shard_map/tpf,fd->tpd/dot_general | solution.py:415
  194.4 0.5 collective-permute-start.5
  194.9 0.1 dynamic-slice_convert_fusion
  194.9 2.5 collective-permute-done.5
  197.5 7.0 %fusion.50 = bf16[2,256,256]{2,1,0:T(8,128)(2,1)} fusion(bf16[2,256,1024]{2,1,0:T(8,128)(2,1)} %copy-done.4, bf16[2,256,1024]{2,1,0:T(8,128)(2,1)} %collective-permute-done.5, bf16[2,256,2048]{2,1,0:T(8,128)(2,1)} %fusion.9, bf16[2048,1024,1]{1,0,2:T(8,128)(2,1)} %bitcast.90, bf16[1024,256]{1,0:T(8,128)(2,1)} %param.20, ...), kind=kOutput, calls=%fused_computation.62 | convolution fusion | flops 2419195904 | bytes 9175044 | tf_op jit(solution)/shard_map/tpd,dc->tpc/dot_general | solution.py:425
  204.5 1.7 copy.79
  206.1 4.1 %all-to-all-start = ((bf16[4,2,64,256]{3,2,1,0:T(8,128)(2,1)}), bf16[4,2,64,256]{3,2,1,0:T(8,128)(2,1)}, u32[]{:S(2)}, u32[]{:S(2)}) async-start(bf16[4,2,64,256]{3,2,1,0:T(8,128)(2,1)} %bitcast.81), calls=%async_computation | async-start | bytes 524288 | tf_op jit(solution)/shard_map/all_to_all | solution.py:430
  210.2 0.1 dynamic_slice.9
  210.3 9.6 %all-to-all-done = bf16[4,2,64,256]{3,2,1,0:T(8,128)(2,1)} async-done(((bf16[4,2,64,256]{3,2,1,0:T(8,128)(2,1)}), bf16[4,2,64,256]{3,2,1,0:T(8,128)(2,1)}, u32[]{:S(2)}, u32[]{:S(2)}) %all-to-all-start) | async-done | bytes 262176 | tf_op jit(solution)/shard_map/all_to_all | solution.py:430
  220.0 1.2 convolution_convert_fusion.4
  221.2 0.8 copy.43
  221.9 4.1 %all-to-all-start.1 = ((bf16[8,64,256]{2,1,0:T(8,128)(2,1)}), bf16[8,64,256]{2,1,0:T(8,128)(2,1)}, u32[]{:S(2)}, u32[]{:S(2)}) async-start(bf16[8,64,256]{2,1,0:T(8,128)(2,1)} %copy.43), calls=%async_computation.1 | async-start | bytes 524288 | tf_op jit(solution)/shard_map/all_to_all | solution.py:452
  226.0 7.0 %all-to-all-done.1 = bf16[8,64,256]{2,1,0:T(8,128)(2,1)} async-done(((bf16[8,64,256]{2,1,0:T(8,128)(2,1)}), bf16[8,64,256]{2,1,0:T(8,128)(2,1)}, u32[]{:S(2)}, u32[]{:S(2)}) %all-to-all-start.1) | async-done | bytes 262176 | tf_op jit(solution)/shard_map/all_to_all | solution.py:452
  233.0 2.1 fusion.54
  235.1 1.0 copy.78.mid_ref
  236.2 2.0 collective-permute-start.6
  238.2 1.3 collective-permute-start.7
  239.4 1.2 collective-permute-done.6.low_ref
  240.6 6.7 %collective-permute-done.7.high_ref = bf16[8,32,256]{2,1,0:T(8,128)(2,1)S(1)} collective-permute-done((bf16[8,32,256]{2,1,0:T(8,128)(2,1)S(1)}, bf16[8,32,256]{2,1,0:T(8,128)(2,1)S(1)}, u32[]{:S(2)}, u32[]{:S(2)}) %collective-permute-start.7) | collective-permute-done | bytes 131104 | tf_op jit(solution)/shard_map/ppermute | solution.py:248
  247.4 17.7 %scene_convolutions.1 = bf16[8,256,256]{2,1,0:T(8,128)(2,1)} custom-call(bf16[8,32,256]{2,1,0:T(8,128)(2,1)S(1)} %collective-permute-done.6.low_ref, bf16[8,64,256]{2,1,0:T(8,128)(2,1)S(1)} %copy.78.mid_ref, bf16[8,32,256]{2,1,0:T(8,128)(2,1)S(1)} %collective-permute-done.7.high_ref, bf16[3,256,256]{2,1,0:T(8,128)(2,1)S(1)} %collective-permute-done.2.guide_low, ...), custom_call_target="tpu_custom_call" | custom-call | tf_op jit(solution)/shard_map/scene_convolutions/pallas_call | solution.py:336
  (39 shorter events, 0.1 us)
Async XLA Ops:
  0.0 1.4 copy-start
  2.4 135.9 %copy-start.6 = (f32[1024]{0:T(1024)S(1)}, f32[1024]{0:T(1024)}, u32[]{:S(2)}) copy-start(f32[1024]{0:T(1024)} %param.14) | copy-start | bytes 12292
  135.1 5.0 %copy-start.1 = (bf16[8,256,256]{2,1,0:T(8,128)(2,1)S(1)}, bf16[8,256,256]{2,1,0:T(8,128)(2,1)}, u32[]{:S(2)}) copy-start(bf16[8,256,256]{2,1,0:T(8,128)(2,1)} %guide_mid.1) | copy-start | bytes 3145732
  135.1 14.1 %copy-start.10 = (bf16[4,3072,128]{2,1,0:T(8,128)(2,1)S(1)}, bf16[4,3072,128]{2,1,0:T(8,128)(2,1)}, u32[]{:S(2)}) copy-start(bf16[4,3072,128]{2,1,0:T(8,128)(2,1)} %get-tuple-element.18) | copy-start | bytes 9437188
  139.9 12.3 %collective-permute-start = (bf16[2,256,1024]{2,1,0:T(8,128)(2,1)S(1)}, bf16[2,256,1024]{2,1,0:T(8,128)(2,1)S(1)}, u32[]{:S(2)}, u32[]{:S(2)}) collective-permute-start(bf16[2,256,1024]{2,1,0:T(8,128)(2,1)S(1)} %fusion.33), channel_id=1, source_target_pairs={{0,4},{4,0},{8,12},{12,8},{16,20},{20,16},{24,28},{28,24},{1,5},{5... | collective-permute-start | bytes 3145736 | tf_op jit(solution)/shard_map/ppermute | solution.py:402
  141.0 36.7 %collective-permute-start.2 = (bf16[3,256,256]{2,1,0:T(8,128)(2,1)}, bf16[3,256,256]{2,1,0:T(8,128)(2,1)S(1)}, u32[]{:S(2)}, u32[]{:S(2)}) collective-permute-start(bf16[3,256,256]{2,1,0:T(8,128)(2,1)} %get-tuple-element.38), channel_id=1, source_target_pairs={{0,1},{1,2},{2,3},{3,4},{4,5},{5,6},{6,7},{7,8},{8,9},{9,10},{10,1... | collective-permute-start | bytes 1179656 | tf_op jit(solution)/shard_map/ppermute | solution.py:247
  147.7 30.1 %collective-permute-start.3 = (bf16[3,256,256]{2,1,0:T(8,128)(2,1)}, bf16[3,256,256]{2,1,0:T(8,128)(2,1)S(1)}, u32[]{:S(2)}, u32[]{:S(2)}) collective-permute-start(bf16[3,256,256]{2,1,0:T(8,128)(2,1)} %get-tuple-element.37), channel_id=1, source_target_pairs={{1,0},{2,1},{3,2},{4,3},{5,4},{6,5},{7,6},{8,7},{9,8},{10,9},{11,1... | collective-permute-start | bytes 1179656 | tf_op jit(solution)/shard_map/ppermute | solution.py:248
  160.0 2.9 %copy-start.11 = (bf16[4,128,1024]{2,1,0:T(8,128)(2,1)S(1)}, bf16[4,128,1024]{2,1,0:T(8,128)(2,1)}, u32[]{:S(2)}) copy-start(bf16[4,128,1024]{2,1,0:T(8,128)(2,1)} %get-tuple-element.20) | copy-start | bytes 3145732
  162.9 3.7 %copy-start.5 = (bf16[3,4,2,256,128]{3,4,2,0,1:T(8,128)(2,1)S(1)}, bf16[3,4,2,256,128]{3,4,2,0,1:T(8,128)(2,1)}, u32[]{:S(2)}) copy-start(bf16[3,4,2,256,128]{3,4,2,0,1:T(8,128)(2,1)} %fusion.42) | copy-start | bytes 4718596
  164.6 10.8 %collective-permute-start.1 = (bf16[2,256,1024]{2,1,0:T(8,128)(2,1)}, bf16[2,256,1024]{2,1,0:T(8,128)(2,1)}, u32[]{:S(2)}, u32[]{:S(2)}) collective-permute-start(bf16[2,256,1024]{2,1,0:T(8,128)(2,1)} %convolution_convert_fusion.2), channel_id=1, source_target_pairs={{0,4},{4,0},{8,12},{12,8},{16,20},{20,16},{24,28},{28,24},{1,5},{5... | collective-permute-start | bytes 3145736 | tf_op jit(solution)/shard_map/ppermute | solution.py:404
  172.4 3.0 %copy-start.3 = (bf16[2,256,1024]{2,1,0:T(8,128)(2,1)S(1)}, bf16[2,256,1024]{2,1,0:T(8,128)(2,1)}, u32[]{:S(2)}) copy-start(bf16[2,256,1024]{2,1,0:T(8,128)(2,1)} %get-tuple-element.17) | copy-start | bytes 3145732
  172.4 3.0 %copy-start.12 = (bf16[4,128,1024]{2,1,0:T(8,128)(2,1)S(1)}, bf16[4,128,1024]{2,1,0:T(8,128)(2,1)}, u32[]{:S(2)}) copy-start(bf16[4,128,1024]{2,1,0:T(8,128)(2,1)} %get-tuple-element.20) | copy-start | bytes 3145732
  175.5 3.2 %copy-start.7 = (f32[1024]{0:T(1024)S(1)}, f32[1024]{0:T(1024)}, u32[]{:S(2)}) copy-start(f32[1024]{0:T(1024)} %param.15) | copy-start | bytes 12292
  175.5 3.7 %copy-start.9 = (bf16[4,512,1024]{2,1,0:T(8,128)(2,1)S(1)}, bf16[4,512,1024]{2,1,0:T(8,128)(2,1)}, u32[]{:S(2)}) copy-start(bf16[4,512,1024]{2,1,0:T(8,128)(2,1)} %get-tuple-element.23) | copy-start | bytes 12582916
  177.7 1.0 copy-start.4
  179.1 4.9 %collective-permute-start.4 = (bf16[2,256,1024]{2,1,0:T(8,128)(2,1)S(1)}, bf16[2,256,1024]{2,1,0:T(8,128)(2,1)S(1)}, u32[]{:S(2)}, u32[]{:S(2)}) collective-permute-start(bf16[2,256,1024]{2,1,0:T(8,128)(2,1)S(1)} %fusion.30), channel_id=1, source_target_pairs={{0,4},{4,0},{8,12},{12,8},{16,20},{20,16},{24,28},{28,24},{1,5},{5... | collective-permute-start | bytes 3145736 | tf_op jit(solution)/shard_map/ppermute | solution.py:417
  184.0 1.0 copy-start.13
  184.9 9.9 %copy-start.14 = (s32[8]{0:T(128)S(1)}, s32[8]{0:T(128)}, u32[]{:S(2)}) copy-start(s32[8]{0:T(128)} %param.21) | copy-start | bytes 100
  194.4 3.1 %collective-permute-start.5 = (bf16[2,256,1024]{2,1,0:T(8,128)(2,1)}, bf16[2,256,1024]{2,1,0:T(8,128)(2,1)}, u32[]{:S(2)}, u32[]{:S(2)}) collective-permute-start(bf16[2,256,1024]{2,1,0:T(8,128)(2,1)} %convolution_convert_fusion.3), channel_id=1, source_target_pairs={{0,4},{4,0},{8,12},{12,8},{16,20},{20,16},{24,28},{28,24},{1,5},{5... | collective-permute-start | bytes 3145736 | tf_op jit(solution)/shard_map/ppermute | solution.py:419
  194.9 15.3 %copy-start.8 = (s32[64]{0:T(128)S(1)}, s32[64]{0:T(128)}, u32[]{:S(2)}) copy-start(s32[64]{0:T(128)} %param.22) | copy-start | bytes 772
  204.5 42.9 %copy-start.2 = (f32[3,256]{1,0:T(4,128)S(1)}, f32[3,256]{1,0:T(4,128)}, u32[]{:S(2)}) copy-start(f32[3,256]{1,0:T(4,128)} %bias_ref.1) | copy-start | bytes 9220
  206.1 13.8 %all-to-all-start = ((bf16[4,2,64,256]{3,2,1,0:T(8,128)(2,1)}), bf16[4,2,64,256]{3,2,1,0:T(8,128)(2,1)}, u32[]{:S(2)}, u32[]{:S(2)}) async-start(bf16[4,2,64,256]{3,2,1,0:T(8,128)(2,1)} %bitcast.81), calls=%async_computation | async-start | bytes 524288 | tf_op jit(solution)/shard_map/all_to_all | solution.py:430
  221.9 11.1 %all-to-all-start.1 = ((bf16[8,64,256]{2,1,0:T(8,128)(2,1)}), bf16[8,64,256]{2,1,0:T(8,128)(2,1)}, u32[]{:S(2)}, u32[]{:S(2)}) async-start(bf16[8,64,256]{2,1,0:T(8,128)(2,1)} %copy.43), calls=%async_computation.1 | async-start | bytes 524288 | tf_op jit(solution)/shard_map/all_to_all | solution.py:452
  236.2 4.5 %collective-permute-start.6 = (bf16[8,32,256]{2,1,0:T(8,128)(2,1)S(1)}, bf16[8,32,256]{2,1,0:T(8,128)(2,1)S(1)}, u32[]{:S(2)}, u32[]{:S(2)}) collective-permute-start(bf16[8,32,256]{2,1,0:T(8,128)(2,1)S(1)} %get-tuple-element.40), channel_id=1, source_target_pairs={{0,1},{1,2},{2,3},{3,4},{4,5},{5,6},{6,7},{7,8},{8,9},{9,10},{10,1... | collective-permute-start | bytes 393224 | tf_op jit(solution)/shard_map/ppermute | solution.py:247
  238.2 9.2 %collective-permute-start.7 = (bf16[8,32,256]{2,1,0:T(8,128)(2,1)S(1)}, bf16[8,32,256]{2,1,0:T(8,128)(2,1)S(1)}, u32[]{:S(2)}, u32[]{:S(2)}) collective-permute-start(bf16[8,32,256]{2,1,0:T(8,128)(2,1)S(1)} %get-tuple-element.39), channel_id=1, source_target_pairs={{1,0},{2,1},{3,2},{4,3},{5,4},{6,5},{7,6},{8,7},{9,8},{10,9},{11,1... | collective-permute-start | bytes 393224 | tf_op jit(solution)/shard_map/ppermute | solution.py:248
